TPU v7x, 256 devices: a whole 4x4x8 slice. The times are simulated.
256 devices in a mesh: dp: 64 (over z, x, core), rep: 4 (over y).
Axes of the slice: x: 4, y: 4, z: 8, core: 2. Of those that a mesh axis runs over, the one named last changes fastest.
Arguments:
- hot_slab: bfloat16 [32768, 128], replicated, may hold values from -3 to 3
- hot_accum: float32 [32768], P(('dp', 'rep')), may hold values from 0.001 to 0.1
- cold_table: float32 [131072, 128], P('dp'), may hold values from -3 to 3
- cold_accum: float32 [131072], P('dp'), may hold values from 0.0001 to 0.01
- touched_owner: int32 [262144, 1], P(('dp', 'rep')), may hold values from 0 to 63; in each aligned block of 1024 rows (0 to 1023, 1024 to 2047, ...) at most 48 rows name the same one
- touched_row: int32 [262144], P(('dp', 'rep')), may hold values from 0 to 2047
- lookup_index: int32 [2097152], P(('dp', 'rep')), may hold values from 0 to 33791
- bag_id: int32 [256, 8192], P(('dp', 'rep')), may hold values from 0 to 2047, never falling along the last dimension, each value on 1 to 16 neighbouring positions
- labels: float32 [65536], P(('dp', 'rep')), may hold values from 0 to 1
- w_hidden: bfloat16 [1024, 1024], replicated, may hold values from -0.1875 to 0.1875
- hidden_accum: float32 [1024, 1024], P(('dp', 'rep')), may hold values from 1 to 30
- w_out: float32 [1024], replicated, may hold values from -0.1875 to 0.1875
- out_accum: float32 [1024], P(('dp', 'rep')), may hold values from 1000 to 30000
Outputs:
- hot_new: float32 [32768, 128], P(('dp', 'rep'))
- hot_accum_new: float32 [32768], P(('dp', 'rep'))
- cold_new: float32 [131072, 128], P('dp')
- cold_accum_new: float32 [131072], P('dp')
- hidden_new: float32 [1024, 1024], P(('dp', 'rep'))
- hidden_accum_new: float32 [1024, 1024], P(('dp', 'rep'))
- out_new: float32 [1024], P(('dp', 'rep'))
- out_accum_new: float32 [1024], P(('dp', 'rep'))
Inputs may be any that keep to these rules, and one draw needn't show every extreme that they name: `touched_owner`: among the 1024 touched rows of one device, no owner is named more than 48 times. `bag_id`: Non-decreasing along each device's lookups; each of the 2048 bags holds 1 to 16 lookups.
All inputs are finite; a program needn't handle non-finite values.
Results may differ from a plain program's by a relative error of at most 0.00035.
Values may be sent and summed in bfloat16 or wider, within the bound.
No kernel may reach another device: no remote copies, remote signals or barrier semaphores. Data moves between devices by JAX's collectives and lax.ppermute only.
A program may use at most 128 MiB of HBM per device.

v0:
```python
import jax
import jax.numpy as jnp
from jax import lax
from jax.sharding import PartitionSpec as P

learn_rate = 0.05


def local_pass(hot_slab, fetched, lookups, bag_ids, targets, w_hidden, w_out):
    hot_count, emb_width = hot_slab.shape
    samples = targets.shape[0]
    input_width = w_hidden.shape[0]
    bag_count = samples * input_width // emb_width
    is_hot = lookups < hot_count
    hot_part = jnp.take(hot_slab, jnp.where(is_hot, lookups, 0), axis=0)
    cold_part = jnp.take(fetched, jnp.where(is_hot, 0, lookups - hot_count), axis=0)
    values = jnp.where(is_hot[:, None], hot_part, cold_part).astype(jnp.float32)
    pooled = jax.ops.segment_sum(values, bag_ids, num_segments=bag_count, indices_are_sorted=True)
    pooled_in = pooled.reshape(samples, input_width).astype(jnp.bfloat16)
    preact = jnp.dot(pooled_in, w_hidden, preferred_element_type=jnp.float32)
    gate_sig = jax.nn.sigmoid(preact)
    hidden_act = (preact * gate_sig).astype(jnp.bfloat16)
    act_wide = hidden_act.astype(jnp.float32)
    logits = jnp.dot(act_wide, w_out, precision=lax.Precision.HIGHEST)
    logit_grad = jax.nn.sigmoid(logits) - targets
    out_grad = jnp.dot(logit_grad, act_wide, precision=lax.Precision.HIGHEST)
    act_grad = (
        logit_grad[:, None] * w_out[None, :] * gate_sig * (1.0 + preact * (1.0 - gate_sig))
    ).astype(jnp.bfloat16)
    hidden_grad = jnp.dot(pooled_in.T, act_grad, preferred_element_type=jnp.float32)
    input_grad = jnp.dot(act_grad, w_hidden.T, preferred_element_type=jnp.float32)
    lookup_grad = jnp.take(input_grad.reshape(bag_count, emb_width), bag_ids, axis=0)
    return (lookup_grad, is_hot, hidden_grad, out_grad)


def row_adagrad(param, accum, grad):
    accum_new = accum + jnp.mean(grad * grad, axis=1)
    return (param - learn_rate * grad / jnp.sqrt(accum_new)[:, None], accum_new)


def elem_adagrad(param, accum, grad):
    accum_new = accum + grad * grad
    return (param - learn_rate * grad / jnp.sqrt(accum_new), accum_new)


def on_device(
    hot_slab,
    hot_accum,
    cold_table,
    cold_accum,
    touched_owner,
    touched_row,
    lookup_index,
    bag_id,
    labels,
    w_hidden,
    hidden_accum,
    w_out,
    out_accum,
):
    hot_count, emb_width = hot_slab.shape
    touched = touched_row.shape[0]
    owners = lax.axis_size("dp")
    capacity = max(2, 3 * touched // owners)
    table_rows = cold_table.shape[0]
    owner_ids = touched_owner[:, 0]
    member = (owner_ids[:, None] == jnp.arange(owners, dtype=jnp.int32)[None, :]).astype(jnp.int32)
    before = jnp.cumsum(member, axis=0) - member
    within = jnp.sum(before * member, axis=1)
    slot_pos = owner_ids * capacity + within
    requests = (
        jnp.full((owners * capacity,), -1, jnp.int32)
        .at[slot_pos]
        .set(touched_row)
        .reshape(owners, capacity)
    )
    asked_rows = lax.all_to_all(requests, "dp", split_axis=0, concat_axis=0, tiled=True)
    clipped = jnp.clip(asked_rows, 0, table_rows - 1)
    found_rows = jnp.take(cold_table, clipped, axis=0).astype(jnp.bfloat16)
    returned = lax.all_to_all(found_rows, "dp", split_axis=0, concat_axis=0, tiled=True)
    returned, asked_rows = (returned, asked_rows)
    fetched = jnp.take(returned.reshape(owners * capacity, emb_width), slot_pos, axis=0)
    lookup_grad, is_hot, hidden_grad, out_grad = local_pass(
        hot_slab, fetched, lookup_index, bag_id[0], labels, w_hidden, w_out
    )
    slot_target = jnp.where(is_hot, touched, lookup_index - hot_count)
    slot_grad = (
        jnp.zeros((touched, emb_width), jnp.float32).at[slot_target].add(lookup_grad, mode="drop")
    )
    outgoing = (
        jnp.zeros((owners * capacity, emb_width), jnp.float32)
        .at[slot_pos]
        .set(slot_grad)
        .reshape(owners, capacity, emb_width)
    )
    incoming = lax.all_to_all(
        outgoing.astype(jnp.bfloat16), "dp", split_axis=0, concat_axis=0, tiled=True
    ).astype(outgoing.dtype)
    owner_target = jnp.where(asked_rows >= 0, asked_rows, table_rows).reshape(-1)
    table_grad = (
        jnp.zeros((table_rows, emb_width), jnp.float32)
        .at[owner_target]
        .add(incoming.reshape(-1, emb_width), mode="drop")
    )
    table_grad = lax.psum(table_grad.astype(jnp.bfloat16), "rep").astype(jnp.float32)
    cold_new, cold_accum_new = row_adagrad(cold_table, cold_accum, table_grad)
    position = lax.axis_index(("dp", "rep"))
    slab_rows = hot_accum.shape[0]
    hot_target = jnp.where(is_hot, lookup_index, hot_count)
    dense_grad = (
        jnp.zeros((hot_count, emb_width), jnp.float32).at[hot_target].add(lookup_grad, mode="drop")
    )
    hot_grad = lax.psum_scatter(dense_grad, ("dp", "rep"), scatter_dimension=0, tiled=True)
    own_slab = lax.dynamic_slice_in_dim(hot_slab, position * slab_rows, slab_rows, 0).astype(
        jnp.float32
    )
    hot_new, hot_accum_new = row_adagrad(own_slab, hot_accum, hot_grad)
    hidden_rows = hidden_accum.shape[0]
    out_rows = out_accum.shape[0]
    hidden_total, out_total = lax.psum((hidden_grad, out_grad), ("dp", "rep"))
    hidden_part = lax.dynamic_slice_in_dim(hidden_total, position * hidden_rows, hidden_rows, 0)
    out_part = lax.dynamic_slice_in_dim(out_total, position * out_rows, out_rows, 0)
    own_hidden = lax.dynamic_slice_in_dim(w_hidden, position * hidden_rows, hidden_rows, 0).astype(
        jnp.float32
    )
    own_out = lax.dynamic_slice_in_dim(w_out, position * out_rows, out_rows, 0)
    hidden_new, hidden_accum_new = elem_adagrad(own_hidden, hidden_accum, hidden_part)
    out_new, out_accum_new = elem_adagrad(own_out, out_accum, out_part)
    return (
        hot_new,
        hot_accum_new,
        cold_new,
        cold_accum_new,
        hidden_new,
        hidden_accum_new,
        out_new,
        out_accum_new,
    )


def solution(mesh):
    in_specs = (
        P(),
        P(("dp", "rep")),
        P("dp", None),
        P("dp"),
        P(("dp", "rep"), None),
        P(("dp", "rep")),
        P(("dp", "rep")),
        P(("dp", "rep"), None),
        P(("dp", "rep")),
        P(),
        P(("dp", "rep"), None),
        P(),
        P(("dp", "rep")),
    )
    out_specs = (
        P(("dp", "rep"), None),
        P(("dp", "rep")),
        P("dp", None),
        P("dp"),
        P(("dp", "rep"), None),
        P(("dp", "rep"), None),
        P(("dp", "rep")),
        P(("dp", "rep")),
    )
    return jax.shard_map(
        on_device, mesh=mesh, in_specs=in_specs, out_specs=out_specs, check_vma=False
    )
```

profile of v0, /device:TPU:2, one launch (start us, length us, event | category | flops | bytes accessed | tf_op | source)
XLA Modules:
  0.0 1973.3 jit_solution(9643238098225158067)
XLA Ops:
  8.0 18.0 reduce-window.6
  28.0 4.5 scatter_custom_fusion
  33.2 12.0 all-to-all-start
  46.8 6.9 all-to-all-done
  55.2 8.3 gather_fusion
  63.5 1.3 select_convert_fusion
  64.8 5.5 all-to-all-start.1
  70.5 23.2 %all-to-all-done.1 = bf16[64,48,128]{2,1,0:T(8,128)(2,1)S(1)} async-done(((bf16[64,48,128]{2,1,0:T(8,128)(2,1)}), bf16[64,48,128]{2,1,0:T(8,128)(2,1)S(1)}, u32[]{:S(2)}, u32[]{:S(2)}) %all-to-all-start.1) | async-done | bytes 786464 | tf_op jit(solution)/shard_map/all_to_all | solution.py:80
  93.6 3.2 gather_fusion.1
  97.1 129.7 %scatter_custom_fusion.1 = f32[2048,128]{1,0:T(8,128)S(1)} fusion(s32[8192]{0:T(1024)S(1)} %bitcast.59, pred[8192]{0:T(1024)(128)(4,1)S(1)} %get-tuple-element.25, pred[8192]{0:T(1024)(128)(4,1)S(1)} %get-tuple-element.26, pred[8192]{0:T(1024)(128)(4,1)S(1)} %get-tuple-element.24, bf16[]{:T(256)} %constant.64.clone.1, f32[]{:T(128)} %constant.59.clone.1, ...), kind=kCustom, calls=%fused_computation.13 | custom fusion | flops 5242880 | bytes 9789446 | tf_op jit(solution)/shard_map/scatter-add | solution.py:18
  227.1 2.6 multiply_convert_fusion.1
  231.1 2.0 fusion.39
  233.1 1.4 reshape.170
  234.5 27.7 %gather_fusion.2 = f32[8192,128]{1,0:T(8,128)} fusion(f32[2048,128]{1,0:T(8,128)S(1)} %reshape.170, s32[8192]{0:T(1024)S(1)} %broadcast_clamp_fusion), kind=kCustom, calls=%fused_computation.4 | custom fusion | bytes 8421376 | tf_op jit(solution)/shard_map/jit(_take)/gather | solution.py:32
  262.2 49.9 %scatter_custom_fusion.3 = f32[1024,128]{1,0:T(8,128)} fusion(s32[8192]{0:T(1024)S(1)} %get-tuple-element.18, f32[8192,128]{1,0:T(8,128)} %gather_fusion.2, f32[]{:T(128)} %constant.84.clone.1, pred[8192]{0:T(1024)(128)(4,1)S(1)} %compare_and_fusion.3, f32[]{:T(128)} %constant.59.clone.1), kind=kCustom, calls=%fused_computation.15 | custom fusion | flops 2097152 | bytes 4726792 | tf_op jit(solution)/shard_map/scatter-add | solution.py:88
  312.1 3.9 scatter_custom_fusion.4
  316.0 1.0 convert_element_type.54
  317.0 5.8 all-to-all-start.2
  322.9 23.0 %all-to-all-done.2 = bf16[64,48,128]{2,1,0:T(8,128)(2,1)S(1)} async-done(((bf16[64,48,128]{2,1,0:T(8,128)(2,1)}), bf16[64,48,128]{2,1,0:T(8,128)(2,1)S(1)}, u32[]{:S(2)}, u32[]{:S(2)}) %all-to-all-start.2) | async-done | bytes 786464 | tf_op jit(solution)/shard_map/all_to_all | solution.py:96
  345.9 17.2 scatter_custom_fusion.5
  363.1 0.8 convert_element_type.56
  364.1 4.2 fusion.38
  368.5 55.9 %scatter_custom_fusion.2 = f32[32768,128]{1,0:T(8,128)} fusion(s32[8192]{0:T(1024)S(1)} %get-tuple-element.19, f32[]{:T(128)} %constant.59.clone.1, f32[8192,128]{1,0:T(8,128)} %gather_fusion.2, f32[]{:T(128)} %constant.84.clone.1, pred[8192]{0:T(1024)(128)(4,1)S(1)} %compare_and_fusion.3), kind=kCustom, calls=%fused_computation.11 | custom fusion | flops 2097152 | bytes 20979720 | tf_op jit(solution)/shard_map/scatter-add | solution.py:111
  424.5 1.0 copy-done.2
  425.8 75.6 %psum.23 = f32[1024]{0:T(1024)S(1)} all-reduce(f32[1024]{0:T(1024)S(1)} %bitcast.66), channel_id=1, replica_groups=mesh['dp'=64,'rep'=4] {'dp','rep'}, use_global_device_ids=true, to_apply=%region_14.15 | all-reduce | flops 1024 | bytes 8192 | tf_op jit(solution)/shard_map/psum | solution.py:120
  501.9 1.4 fusion.21
  503.9 2.4 fusion.20
  506.3 177.9 %all-reduce.5.cloned.1.call-done = f32[1024,1024]{1,0:T(8,128)} async-done(((f32[1024,1024]{1,0:T(8,128)}), f32[1024,1024]{1,0:T(8,128)}) %all-reduce.5.cloned.1.call-update) | async-done | bytes 4194320 | tf_op jit(solution)/shard_map/psum | solution.py:120
  684.2 1.4 multiply_subtract_fusion
  685.6 1278.2 %reduce-scatter.2.cloned.1.call-done = f32[128,128]{1,0:T(8,128)} async-done(((f32[32768,128]{1,0:T(8,128)}), f32[128,128]{1,0:T(8,128)}) %reduce-scatter.2.cloned.1.call-update) | async-done | bytes 65552 | tf_op jit(solution)/shard_map/reduce_scatter | solution.py:113
  1963.8 0.9 multiply_reduce_fusion
  1965.2 1.6 divide_subtract_fusion
  (65 shorter events, 10.9 us)
Async XLA Ops:
  7.2 48.0 %copy-start = (f32[2048,128]{1,0:T(8,128)S(1)}, f32[2048,128]{1,0:T(8,128)}, u32[]{:S(2)}) copy-start(f32[2048,128]{1,0:T(8,128)} %param.15) | copy-start | bytes 3145732
  33.2 20.5 %all-to-all-start = ((s32[64,1,48]{2,1,0:T(1,128)}), s32[64,1,48]{2,1,0:T(1,128)S(1)}, u32[]{:S(2)}, u32[]{:S(2)}) async-start(s32[64,1,48]{2,1,0:T(1,128)} %bitcast.7), calls=%async_computation | async-start | bytes 65536 | tf_op jit(solution)/shard_map/all_to_all | solution.py:77
  55.2 15.2 copy-start.5
  55.2 15.3 copy-start.4
  64.8 28.8 %all-to-all-start.1 = ((bf16[64,48,128]{2,1,0:T(8,128)(2,1)}), bf16[64,48,128]{2,1,0:T(8,128)(2,1)S(1)}, u32[]{:S(2)}, u32[]{:S(2)}) async-start(bf16[64,48,128]{2,1,0:T(8,128)(2,1)} %select_convert_fusion), calls=%async_computation.1 | async-start | bytes 1572864 | tf_op jit(solution)/shard_map/all_to_all | solution.py:80
  226.8 3.7 copy-start.6
  227.1 3.9 copy-start.9
  227.1 4.0 copy-start.12
  229.7 0.8 copy-start.1
  229.7 1.4 copy-start.3
  317.0 29.0 %all-to-all-start.2 = ((bf16[64,48,128]{2,1,0:T(8,128)(2,1)}), bf16[64,48,128]{2,1,0:T(8,128)(2,1)S(1)}, u32[]{:S(2)}, u32[]{:S(2)}) async-start(bf16[64,48,128]{2,1,0:T(8,128)(2,1)} %bitcast.54), calls=%async_computation.3 | async-start | bytes 1572864 | tf_op jit(solution)/shard_map/all_to_all | solution.py:96
  322.7 179.2 %all-reduce.3.cloned.1.call-start = ((), (), s32[]{:S(2)}) async-start(), calls=%async_computation.5 | async-start | bytes 1048576 | tf_op jit(solution)/shard_map/psum | solution.py:105
  364.0 320.2 %all-reduce.5.cloned.1.call-start = ((), (), s32[]{:S(2)}) async-start(), calls=%async_computation.6 | async-start | bytes 8388608 | tf_op jit(solution)/shard_map/psum | solution.py:120
  368.3 1595.5 %reduce-scatter.2.cloned.1.call-start = ((), (), s32[]{:S(2)}) async-start(), calls=%async_computation.4 | async-start | bytes 16842752 | tf_op jit(solution)/shard_map/reduce_scatter | solution.py:113
  424.4 1.0 copy-start.2
  424.4 76.9 %copy-start.10 = (f32[4]{0:T(128)S(1)}, f32[4]{0:T(128)}, u32[]{:S(2)}) copy-start(f32[4]{0:T(128)} %param.25) | copy-start | bytes 52
  424.4 78.9 %copy-start.8 = (f32[2048]{0:T(1024)S(1)}, f32[2048]{0:T(1024)}, u32[]{:S(2)}) copy-start(f32[2048]{0:T(1024)} %param.16) | copy-start | bytes 24580
  424.4 259.8 %copy-start.7 = (f32[4,1024]{1,0:T(4,128)S(1)}, f32[4,1024]{1,0:T(4,128)}, u32[]{:S(2)}) copy-start(f32[4,1024]{1,0:T(4,128)} %param.23) | copy-start | bytes 49156
  424.4 1540.3 %copy-start.11 = (f32[128]{0:T(128)S(1)}, f32[128]{0:T(128)}, u32[]{:S(2)}) copy-start(f32[128]{0:T(128)} %param.14) | copy-start | bytes 1540
Sparse Core Ops, SparseCore 0:
  364.1 44.9 all-reduce.2
  414.6 269.5 all-reduce.4
  686.9 1276.8 reduce-scatter.1
where the time goes:
time: 1990 us; the launch traced here: 1970 us
  waiting for transfers between devices  1510 us (76%)
  other arithmetic  288 us (14%)
  blocking collectives  75.6 us (4%)
  local copies, waits for them, and re-layouts  52.8 us (3%)
  starting transfers between devices  23.7 us (1%)
    reduce_scatter x1, waiting for transfers between devices, on_device(): lax.psum_scatter(dense_grad, ('dp', 'rep'), scatter_dimension=0, tiled=True)  1280 us
    psum x1, waiting for transfers between devices, on_device(): hidden_total, out_total = lax.psum((hidden_grad, out_grad), ('dp', 'rep'))  178 us
    scatter-add x1, other arithmetic, local_pass(): jax.ops.segment_sum(values, bag_ids, num_segments=bag_count, indices_are_...  130 us
    psum x1, blocking collectives, on_device(): hidden_total, out_total = lax.psum((hidden_grad, out_grad), ('dp', 'rep'))  75.6 us
    scatter-add x1, other arithmetic, on_device(): jnp.zeros((hot_count, emb_width), jnp.float32).at[hot_target]  55.9 us
    scatter-add x1, other arithmetic, on_device(): jnp.zeros((touched, emb_width), jnp.float32).at[slot_target]  49.9 us
  transfers between devices with their start and end apart: 6, of which 5 were waited for; matrix products, arithmetic and copies ran while one was open for 3% of the time, Pallas kernels for 0%

commit v1 on v0

v1 whole, which is shorter than its diff:
```python
import jax
import jax.numpy as jnp
from jax import lax
from jax.experimental import pallas as pl
from jax.experimental.pallas import tpu as pltpu
from jax.sharding import PartitionSpec as P

learn_rate = 0.05
bf16 = jnp.bfloat16
f32 = jnp.float32
i32 = jnp.int32

EMB = 128
HOT = 32768
FEAT = 8
HID = 1024
B_DEV = 256
BAGS = 2048
LOOK = 8192
UNIQ = 1024
CAP = 48
R_OWN = 2048
N_DP = 64
SLOTS = N_DP * CAP
GROUP = 16
BLOCK = 256
WINDOW = BLOCK + 16
BLOCKS = LOOK // BLOCK
BATCH = 4
PADDED = BAGS + WINDOW
MIB = 1 << 20

ORDERS = ((3, 2, 1, 0), (2, 3, 0, 1), (1, 0, 3, 2), (0, 1, 2, 3))

SMEM = pl.BlockSpec(memory_space=pltpu.SMEM)
VMEM = pl.BlockSpec(memory_space=pltpu.VMEM)
HBM = pl.BlockSpec(memory_space=pltpu.HBM)


def params(mib):
    return pltpu.CompilerParams(vmem_limit_bytes=mib * MIB)


def cost(flops, data):
    return pl.CostEstimate(flops=flops, bytes_accessed=data, transcendentals=0)


def shape(dims, dtype):
    return jax.ShapeDtypeStruct(dims, dtype)


def mm(a, b):
    return jnp.dot(a, b, preferred_element_type=f32)


def mm_nt(a, b):
    return lax.dot_general(a, b, (((1,), (1,)), ((), ())), preferred_element_type=f32)


def mm_tn(a, b):
    return lax.dot_general(a, b, (((0,), (0,)), ((), ())), preferred_element_type=f32)


def route_kernel(owner_ref, row_ref, look_ref, request_ref, pos_ref, clash_ref):
    owner = owner_ref[...]
    row = row_ref[...] + 1
    member = lax.broadcasted_iota(i32, (N_DP, UNIQ), 0) == owner
    ones = member.astype(f32).astype(bf16)
    upper = lax.broadcasted_iota(i32, (UNIQ, UNIQ), 0) < lax.broadcasted_iota(
        i32, (UNIQ, UNIQ), 1
    )
    before = mm(ones, upper.astype(f32).astype(bf16))
    within = jnp.sum(jnp.where(member, before, 0.0), axis=0, keepdims=True).astype(i32)
    pos_ref[...] = owner * CAP + within
    place = (lax.broadcasted_iota(i32, (CAP, UNIQ), 0) == within).astype(f32).astype(bf16)
    high = jnp.where(member, (row >> 6).astype(f32), 0.0).astype(bf16)
    low = jnp.where(member, (row & 63).astype(f32), 0.0).astype(bf16)
    total = mm_nt(high, place) * 64.0 + mm_nt(low, place)
    request_ref[...] = total.astype(i32) - 1
    look = look_ref[...]
    rows = LOOK // 128
    lane = lax.broadcasted_iota(i32, (rows, 128), 1) & (GROUP - 1)
    clash = jnp.zeros((rows, 128), f32)
    for shift in range(1, GROUP):
        same = (look == pltpu.roll(look, shift, 1)) & (lane >= shift)
        clash = jnp.maximum(clash, same.astype(f32))
    group = lax.broadcasted_iota(i32, (128, 128 // GROUP), 0) // GROUP
    gather = group == lax.broadcasted_iota(i32, (128, 128 // GROUP), 1)
    clash_ref[...] = mm(clash.astype(bf16), gather.astype(f32).astype(bf16)).astype(i32)


def route(owner, row, look):
    return pl.pallas_call(
        route_kernel,
        out_shape=(
            shape((N_DP, CAP), i32),
            shape((1, UNIQ), i32),
            shape((LOOK // 128, 128 // GROUP), i32),
        ),
        in_specs=[VMEM] * 3,
        out_specs=[VMEM] * 3,
        compiler_params=params(16),
        name="route",
    )(owner, row, look)


def found_kernel(asked_ref, table_ref, found_ref, rows_ref):
    def body(k, _):
        for j in range(16):
            at = k * 16 + j
            rows_ref[pl.ds(at, 1), :] = table_ref[pl.ds(asked_ref[at], 1), :]
        return 0

    lax.fori_loop(0, SLOTS // 16, body, 0)
    found_ref[...] = rows_ref[...].astype(bf16)


def found_rows(asked, table):
    return pl.pallas_call(
        found_kernel,
        out_shape=shape((SLOTS, EMB), bf16),
        in_specs=[SMEM, VMEM],
        out_specs=VMEM,
        scratch_shapes=[pltpu.VMEM((SLOTS, EMB), f32)],
        compiler_params=params(16),
        name="found",
    )(asked, table)


def counts_kernel(first_ref, look_ref, bag_ref, counts_ref, acc_ref):
    acc_ref[...] = jnp.zeros_like(acc_ref)

    def body(k, _):
        start, in_bag = bags_of(first_ref, bag_ref, k)
        slots = look_ref[pl.ds(k, 1), :] - HOT
        in_slot = (lax.broadcasted_iota(i32, (UNIQ, BLOCK), 0) == slots).astype(f32).astype(bf16)
        acc_ref[pl.ds(start, WINDOW), :] += mm_nt(in_bag, in_slot)
        return 0

    lax.fori_loop(0, BLOCKS, body, 0)
    counts_ref[...] = acc_ref[0:BAGS, :].astype(bf16)


def slot_counts(first, look, bags):
    return pl.pallas_call(
        counts_kernel,
        out_shape=shape((BAGS, UNIQ), bf16),
        in_specs=[SMEM, VMEM, VMEM],
        out_specs=VMEM,
        scratch_shapes=[pltpu.VMEM((PADDED, UNIQ), f32)],
        compiler_params=params(18),
        cost_estimate=cost(5 * 10**9, 8 * MIB),
        name="counts",
    )(first, look, bags)


def bags_of(first_ref, bag_ref, k):
    start = pl.multiple_of((first_ref[k] // 16) * 16, 16)
    bags = bag_ref[pl.ds(k, 1), :] - start
    in_bag = lax.broadcasted_iota(i32, (WINDOW, BLOCK), 0) == bags
    return start, in_bag.astype(f32).astype(bf16)


CHUNKS = 8


def pool_kernel(
    first_ref, look_ref, bag_ref, slab_ref, pooled_ref, slab_vmem, table_ref, rows_ref, acc_ref, sems
):
    height = HOT // CHUNKS

    def copy(c):
        rows = pl.ds(c * height, height)
        return pltpu.make_async_copy(slab_ref.at[rows], slab_vmem.at[rows], sems.at[c])

    for c in range(CHUNKS):
        copy(c).start()
    acc_ref[...] = jnp.zeros_like(acc_ref)
    table_ref[HOT:, :] = jnp.zeros((GROUP, EMB), f32)
    for c in range(CHUNKS):
        copy(c).wait()

        def widen(q, _, c=c):
            rows = pl.ds(pl.multiple_of(c * height + q * 512, 512), 512)
            table_ref[rows, :] = slab_vmem[rows, :].astype(f32)
            return 0

        lax.fori_loop(0, height // 512, widen, 0)

    def gather(q, _):
        for j in range(32):
            at = q * 32 + j
            rows_ref[pl.ds(at, 1), :] = table_ref[pl.ds(look_ref[at], 1), :]
        return 0

    lax.fori_loop(0, LOOK // 32, gather, 0)

    def batch(q, _):
        parts = []
        for j in range(BATCH):
            k = q * BATCH + j
            start, in_bag = bags_of(first_ref, bag_ref, k)
            rows = rows_ref[pl.ds(pl.multiple_of(k * BLOCK, BLOCK), BLOCK), :].astype(bf16)
            parts.append((start, mm(in_bag, rows)))
        for start, part in parts:
            acc_ref[pl.ds(start, WINDOW), :] += part
        return 0

    lax.fori_loop(0, BLOCKS // BATCH, batch, 0)
    pooled_ref[...] = acc_ref[0:BAGS, :]


def pool_hot(first, look, bags, slab):
    return pl.pallas_call(
        pool_kernel,
        out_shape=shape((BAGS, EMB), f32),
        in_specs=[SMEM, SMEM, VMEM, HBM],
        out_specs=VMEM,
        scratch_shapes=[
            pltpu.VMEM((HOT, EMB), bf16),
            pltpu.VMEM((HOT + GROUP, EMB), f32),
            pltpu.VMEM((LOOK, EMB), f32),
            pltpu.VMEM((PADDED, EMB), f32),
            pltpu.SemaphoreType.DMA((CHUNKS,)),
        ],
        compiler_params=params(33),
        cost_estimate=cost(10**9, 40 * MIB),
        name="pool",
    )(first, look, bags, slab)


def layer_kernel(
    pos_ref,
    pooled_ref,
    counts_ref,
    returned_ref,
    target_ref,
    weight_ref,
    out_weight_ref,
    bag_grad_ref,
    outgoing_ref,
    factors_ref,
    out_grad_ref,
    wide_ref,
    slots_ref,
):
    wide_ref[...] = returned_ref[...].astype(f32)

    def fetch(k, _):
        for j in range(16):
            at = k * 16 + j
            slots_ref[pl.ds(at, 1), :] = wide_ref[pl.ds(pos_ref[at], 1), :]
        return 0

    lax.fori_loop(0, UNIQ // 16, fetch, 0)
    counts = counts_ref[...]
    bag_grad_ref[...] = pooled_ref[...] + mm(counts, slots_ref[...].astype(bf16))
    pooled_in = jnp.concatenate(
        [bag_grad_ref[pl.ds(f, B_DEV, stride=FEAT), :] for f in range(FEAT)], axis=1
    ).astype(bf16)
    weight = weight_ref[...]
    out_weight = out_weight_ref[...]
    preact = mm(pooled_in, weight)
    gate = jax.nn.sigmoid(preact)
    act = (preact * gate).astype(bf16).astype(f32)
    logits = jnp.sum(act * out_weight, axis=1, keepdims=True)
    logit_grad = jax.nn.sigmoid(logits) - target_ref[...]
    out_grad_ref[...] = jnp.sum(act * logit_grad, axis=0, keepdims=True)
    act_grad = (logit_grad * out_weight * gate * (1.0 + preact * (1.0 - gate))).astype(bf16)
    factors_ref[0] = pooled_in
    factors_ref[1] = act_grad
    input_grad = mm_nt(act_grad, weight)
    for f in range(FEAT):
        bag_grad_ref[pl.ds(f, B_DEV, stride=FEAT), :] = input_grad[:, f * EMB : (f + 1) * EMB]

    grads = bag_grad_ref[...]
    high = grads.astype(bf16)
    low = (grads - high.astype(f32)).astype(bf16)
    both = mm_tn(counts, jnp.concatenate([high, low], axis=1))
    slots_ref[...] = both[:, :EMB] + both[:, EMB:]
    wide_ref[...] = jnp.zeros_like(wide_ref)

    def put(k, _):
        for j in range(16):
            at = k * 16 + j
            wide_ref[pl.ds(pos_ref[at], 1), :] = slots_ref[pl.ds(at, 1), :]
        return 0

    lax.fori_loop(0, UNIQ // 16, put, 0)
    outgoing_ref[...] = wide_ref[...].astype(bf16)


def layer(pos, pooled, counts, returned, target, weight, out_weight):
    return pl.pallas_call(
        layer_kernel,
        out_shape=(
            shape((BAGS, EMB), f32),
            shape((SLOTS, EMB), bf16),
            shape((2, B_DEV, HID), bf16),
            shape((1, HID), f32),
        ),
        in_specs=[SMEM] + [VMEM] * 6,
        out_specs=[VMEM] * 4,
        scratch_shapes=[pltpu.VMEM((SLOTS, EMB), f32), pltpu.VMEM((UNIQ, EMB), f32)],
        compiler_params=params(30),
        cost_estimate=cost(4 * 10**9, 20 * MIB),
        name="layer",
    )(pos, pooled, counts, returned, target, weight, out_weight)


def hidden_kernel(mine_ref, one_ref, two_ref, hidden_ref):
    at = lax.broadcasted_iota(i32, (1, HID // 2), 1) ^ mine_ref[0]
    x_high, y_high = (at >> 8) & 1, (at >> 6) & 1
    x = 2 * x_high + (x_high ^ ((at >> 7) & 1))
    y = 2 * y_high + (y_high ^ ((at >> 5) & 1))
    source = ((((at >> 2) & 7) * 4 + x) * 2 + (at >> 9)) * 16 + y * 4 + (at & 3)
    order = (lax.broadcasted_iota(i32, (HID, HID // 2), 0) == source).astype(f32).astype(bf16)
    total = mm_tn(mm(one_ref[0], order).astype(bf16), one_ref[1])
    hidden_ref[...] = total + mm_tn(mm(two_ref[0], order).astype(bf16), two_ref[1])


def hidden_half(mine, one, two):
    return pl.pallas_call(
        hidden_kernel,
        out_shape=shape((HID // 2, HID), f32),
        in_specs=[SMEM, VMEM, VMEM],
        out_specs=VMEM,
        compiler_params=params(24),
        cost_estimate=cost(4 * 10**9, 4 * MIB),
        name="hidden_half",
    )(mine, one, two)


def scatter_kernel(
    look_ref, clash_ref, clashes_ref, first_ref, mine_ref, bag_ref, grad_ref, keep_ref, send_ref, acc_ref, halves_ref, rows_ref
):
    grads = grad_ref[...]
    high, low = split(grads)
    halves_ref[0:BAGS, 0:EMB] = high
    halves_ref[0:BAGS, EMB:] = low
    halves_ref[BAGS:, :] = jnp.zeros((PADDED - BAGS, 2 * EMB), bf16)

    def stage(q, _):
        for j in range(BATCH):
            k = q * BATCH + j
            start, in_bag = bags_of(first_ref, bag_ref, k)
            both = mm_tn(in_bag, halves_ref[pl.ds(start, WINDOW), :])
            rows_ref[pl.ds(pl.multiple_of(k * BLOCK, BLOCK), BLOCK), :] = (
                both[:, :EMB] + both[:, EMB:]
            )
        acc_rows = HOT // (BLOCKS // BATCH)
        for j in range(acc_rows // 512):
            acc_ref[pl.ds(pl.multiple_of(q * acc_rows + j * 512, 512), 512), :] = jnp.zeros(
                (512, EMB), f32
            )
        return 0

    lax.fori_loop(0, BLOCKS // BATCH, stage, 0)

    def distinct(at):
        rows = [look_ref[at + m] for m in range(GROUP)]
        sums = [
            acc_ref[pl.ds(rows[m], 1), :] + rows_ref[pl.ds(at + m, 1), :] for m in range(GROUP)
        ]
        for m in range(GROUP):
            acc_ref[pl.ds(rows[m], 1), :] = sums[m]

    def block(k, _):
        @pl.when(clashes_ref[k] == 0)
        def _():
            def pair(q, _):
                distinct(k * BLOCK + q * 2 * GROUP)
                distinct(k * BLOCK + q * 2 * GROUP + GROUP)
                return 0

            lax.fori_loop(0, BLOCK // GROUP // 2, pair, 0)

        @pl.when(clashes_ref[k] != 0)
        def _():
            def group(q, _):
                at = k * BLOCK + q * GROUP
                clash = clash_ref[k * (BLOCK // GROUP) + q]

                @pl.when(clash == 0)
                def _():
                    distinct(at)

                @pl.when(clash != 0)
                def _():
                    for m in range(GROUP):
                        acc_ref[pl.ds(look_ref[at + m], 1), :] += rows_ref[pl.ds(at + m, 1), :]

                return 0

            lax.fori_loop(0, BLOCK // GROUP, group, 0)

        return 0

    lax.fori_loop(0, BLOCKS, block, 0)

    core, bits = mine_ref[1], mine_ref[2]
    for s in range(4):

        def gather(k, _, s=s):
            bit = [(bits >> (3 - axis)) & 1 for axis in range(4)]
            for j, axis in enumerate(ORDERS[s]):
                bit[axis] = bit[axis] ^ ((k >> (3 - j)) & 1)
            x = 2 * bit[0] + (bit[0] ^ bit[1])
            y = 2 * bit[2] + (bit[2] ^ bit[3])
            base = x * 1024 + y * 128 + 32 * s
            own = pl.multiple_of(base + 512 * core, 32)
            other = pl.multiple_of(base + 512 * (1 - core), 32)
            for z in range(8):
                keep_ref[s, k, z] = acc_ref[pl.ds(own + z * 4096, 32), :]
                send_ref[s, k, z] = acc_ref[pl.ds(other + z * 4096, 32), :].astype(bf16)
            return 0

        lax.fori_loop(0, 16, gather, 0)


def scatter_hot(look, clash, clashes, first, mine, bags, grads):
    return pl.pallas_call(
        scatter_kernel,
        out_shape=(shape((4, 16, 8, 32, EMB), f32), shape((4, 16, 8, 32, EMB), bf16)),
        in_specs=[SMEM] * 5 + [VMEM] * 2,
        out_specs=[VMEM] * 2,
        scratch_shapes=[
            pltpu.VMEM((HOT + GROUP, EMB), f32),
            pltpu.VMEM((PADDED, 2 * EMB), bf16),
            pltpu.VMEM((LOOK, EMB), f32),
        ],
        compiler_params=params(40),
        cost_estimate=cost(10**9, 80 * MIB),
        name="scatter",
    )(look, clash, clashes, first, mine, bags, grads)


def split(values):
    high = values.astype(bf16)
    return high, (values - high.astype(f32)).astype(bf16)


def hot_parts(count):
    return 2 if count <= 2 else 1


def put_hot(send_ref, count, at, total):
    if hot_parts(count) == 2:
        high, low = split(total)
        send_ref[count * 256 + at * 256 : count * 256 + at * 256 + 256, :] = low
    else:
        high = total.astype(bf16)
    send_ref[at * 256 : at * 256 + 256, :] = high


def get_hot(recv_ref, count, at):
    high = recv_ref[at * 256 : at * 256 + 256, :].astype(f32)
    if hot_parts(count) == 2:
        base = count * 256 + at * 256
        high = high + recv_ref[base : base + 256, :].astype(f32)
    return high


def hidden_base(count):
    return count * 256 * hot_parts(count)


def put_hidden(send_ref, count, at, total):
    high, low = split(total)
    base = hidden_base(count) + at * 128
    for part, values in enumerate((high, low)):
        for half in range(2):
            row = base + part * 64 + half * 32
            send_ref[row : row + 32, :] = values[:, half * 128 : half * 128 + 128]


def get_hidden(recv_ref, count, at):
    base = hidden_base(count) + at * 128
    pieces = [recv_ref[base + 32 * q : base + 32 * q + 32, :].astype(f32) for q in range(4)]
    return jnp.concatenate([pieces[0] + pieces[2], pieces[1] + pieces[3]], axis=1)


def out_base(count):
    return hidden_base(count) + count * 128


def put_out(send_ref, count, total):
    high = total.astype(bf16).astype(f32)
    send_ref[out_base(count) : out_base(count) + 16, :] = jnp.concatenate(
        [high, total - high], axis=0
    ).astype(bf16)


def get_out(recv_ref, count):
    wide = recv_ref[out_base(count) : out_base(count) + 16, :].astype(f32)
    return wide[0:8] + wide[8:16]


def rounded_out(total):
    high = total.astype(bf16).astype(f32)
    return high + (total - high).astype(bf16).astype(f32)


def place_of(s, step, k):
    left = sorted(ORDERS[s][step:])
    bit = len(left) - 1 - left.index(ORDERS[s][step])
    rest = ((k >> (bit + 1)) << bit) | (k & ((1 << bit) - 1))
    return (k >> bit) & 1, rest


def send_shapes(count):
    return tuple(
        shape((out_base(count) + (16 if s == 0 else 0), EMB), bf16) for s in range(4)
    ) + (shape((8, EMB), f32),)


def keep_shapes(count):
    return tuple(shape((count, 8, 32, EMB), f32) for s in range(4)) + tuple(
        shape((count, 32, 256), f32) for s in range(4)
    )


def first_send_kernel(keep_ref, recv_ref, hidden_ref, out_ref, out_recv_ref, *outs):
    for s in range(4):

        def hot(k, _, s=s):
            total = keep_ref[s, k + 8].reshape(256, EMB) + recv_ref[s, k + 8].astype(f32).reshape(
                256, EMB
            )
            outs[s][pl.ds(pl.multiple_of(k * 256, 256), 256), :] = total.astype(bf16)
            return 0

        lax.fori_loop(0, 8, hot, 0)
        for k in range(16):
            flag, rest = place_of(s, 0, k)
            if flag:
                put_hidden(
                    outs[s], 8, rest, hidden_ref[32 * k : 32 * k + 32, 256 * s : 256 * s + 256]
                )
    total = out_ref[...] + out_recv_ref[...]
    outs[4][...] = total
    put_out(outs[0], 8, total)


def first_send(keep, recv, hidden, out, out_recv):
    return pl.pallas_call(
        first_send_kernel,
        out_shape=send_shapes(8),
        in_specs=[VMEM] * 5,
        out_specs=[VMEM] * 5,
        compiler_params=params(24),
        cost_estimate=cost(10**6, 12 * MIB),
        name="first_send",
    )(keep, recv, hidden, out, out_recv)


def first_keep_kernel(keep_ref, recv_ref, hidden_ref, *outs):
    for s in range(4):

        def hot(k, _, s=s):
            outs[s][k] = keep_ref[s, k] + recv_ref[s, k].astype(f32)
            return 0

        lax.fori_loop(0, 8, hot, 0)
        for k in range(16):
            flag, rest = place_of(s, 0, k)
            if not flag:
                outs[4 + s][rest] = hidden_ref[32 * k : 32 * k + 32, 256 * s : 256 * s + 256]


def first_keep(keep, recv, hidden):
    return pl.pallas_call(
        first_keep_kernel,
        out_shape=keep_shapes(8),
        in_specs=[VMEM] * 3,
        out_specs=[VMEM] * 8,
        compiler_params=params(24),
        cost_estimate=cost(10**6, 12 * MIB),
        name="first_keep",
    )(keep, recv, hidden)


def next_kernel(step, *refs):
    count = 16 >> step
    recvs, out_ref, hots, hiddens = refs[0:4], refs[4], refs[5:9], refs[9:13]
    sends, out_new_ref, hot_outs, hidden_outs = refs[13:17], refs[17], refs[18:22], refs[22:26]
    for s in range(4):
        for k in range(count):
            total = hots[s][k].reshape(256, EMB) + get_hot(recvs[s], count, k)
            if k >= count // 2:
                put_hot(sends[s], count // 2, k - count // 2, total)
            else:
                hot_outs[s][k] = total.reshape(8, 32, EMB)
            flag, rest = place_of(s, step, k)
            hidden = hiddens[s][k] + get_hidden(recvs[s], count, k)
            if flag:
                put_hidden(sends[s], count // 2, rest, hidden)
            else:
                hidden_outs[s][rest] = hidden
    total = rounded_out(out_ref[...]) + get_out(recvs[0], count)
    out_new_ref[...] = total
    put_out(sends[0], count // 2, total)


def next_step(step, sends, keeps):
    count = 16 >> step
    values = pl.pallas_call(
        lambda *refs: next_kernel(step, *refs),
        out_shape=send_shapes(count // 2) + keep_shapes(count // 2),
        in_specs=[VMEM] * 13,
        out_specs=[VMEM] * 13,
        compiler_params=params(24),
        cost_estimate=cost(10**6, count * 2 * MIB),
        name="step_" + str(step + 1),
    )(*sends, *keeps)
    return values[:5], values[5:]


Z_ROWS = 336


def last_kernel(*refs):
    recvs, sum_ref, hots, hiddens, out_ref, pieces_ref = (
        refs[0:4], refs[4], refs[5:9], refs[9:13], refs[13], refs[14],
    )
    for s in range(4):
        total = hots[s][0].reshape(256, EMB) + get_hot(recvs[s], 1, 0)
        hidden = hiddens[s][0] + get_hidden(recvs[s], 1, 0)
        high, low = split(total)
        for z in range(8):
            out_ref[z, 32 * s : 32 * s + 32, :] = high[32 * z : 32 * z + 32]
            out_ref[z, 128 + 32 * s : 160 + 32 * s, :] = low[32 * z : 32 * z + 32]
            for half in range(2):
                row = (2 * s + half) * 4
                pieces_ref[z, row : row + 4, :] = hidden[
                    4 * z : 4 * z + 4, half * 128 : half * 128 + 128
                ]
    total = rounded_out(sum_ref[...]) + get_out(recvs[0], 1)
    high = total.astype(bf16).astype(f32)
    both = jnp.concatenate([high, total - high], axis=0).astype(bf16)
    for z in range(8):
        high, low = split(pieces_ref[z])
        out_ref[z, 256:288, :] = high
        out_ref[z, 288:320, :] = low
        out_ref[z, 320:336, :] = both


def last_step(sends, keeps):
    return pl.pallas_call(
        last_kernel,
        out_shape=shape((8, Z_ROWS, EMB), bf16),
        in_specs=[VMEM] * 13,
        out_specs=VMEM,
        scratch_shapes=[pltpu.VMEM((8, 32, EMB), f32)],
        compiler_params=params(16),
        cost_estimate=cost(10**6, 2 * MIB),
        name="step_5",
    )(*sends, *keeps)


def row_update(param, accum_row, grad):
    turned = grad.T
    accum_new = accum_row + jnp.sum(turned * turned, axis=0, keepdims=True) * (1.0 / EMB)
    return param - (learn_rate * turned / jnp.sqrt(accum_new)).T, accum_new


def update_kernel(
    recv_ref, slab_ref, accum_ref, weight_ref, hid_accum_ref, new_ref, accum_new_ref, weight_new_ref, hid_new_ref, out_ref
):
    total = jnp.sum(recv_ref[...].astype(f32), axis=0)
    new_ref[...], accum_new_ref[...] = row_update(
        slab_ref[...].astype(f32), accum_ref[...], total[0:128] + total[128:256]
    )
    hidden = total[256:288] + total[288:320]
    for part in range(8):
        columns = slice(part * 128, part * 128 + 128)
        grad = hidden[part * 4 : part * 4 + 4]
        accum_new = hid_accum_ref[:, columns] + grad * grad
        hid_new_ref[:, columns] = accum_new
        weight_new_ref[:, columns] = weight_ref[:, columns] - learn_rate * grad / jnp.sqrt(accum_new)
    out_ref[...] = total[320:328] + total[328:336]


def update_owned(recv, slab, accum, weight, hid_accum):
    return pl.pallas_call(
        update_kernel,
        out_shape=(
            shape((128, EMB), f32),
            shape((1, 128), f32),
            shape((4, HID), f32),
            shape((4, HID), f32),
            shape((8, EMB), f32),
        ),
        in_specs=[VMEM] * 5,
        out_specs=[VMEM] * 5,
        compiler_params=params(16),
        name="update",
    )(recv, slab, accum, weight, hid_accum)


def cold_grad_kernel(asked_ref, incoming_ref, a_ref, b_ref):
    asked = asked_ref[...]
    incoming = incoming_ref[...]
    for part in range(8):
        rows = lax.broadcasted_iota(i32, (256, SLOTS), 0) + part * 256
        total = mm((rows == asked).astype(f32).astype(bf16), incoming).astype(bf16)
        if part < 4:
            a_ref[part * 256 : part * 256 + 256, :] = total
        else:
            b_ref[part * 256 - 1024 : part * 256 - 768, :] = total


def cold_grads(asked, incoming):
    return pl.pallas_call(
        cold_grad_kernel,
        out_shape=(shape((1024, EMB), bf16),) * 2,
        in_specs=[VMEM] * 2,
        out_specs=[VMEM] * 2,
        compiler_params=params(24),
        cost_estimate=cost(2 * 10**9, 4 * MIB),
        name="cold_grads",
    )(asked, incoming)


def pair_kernel(a, b, c, d, e_ref, f_ref):
    e_ref[...] = (a[...].astype(f32) + b[...].astype(f32)).astype(bf16)
    f_ref[...] = (c[...].astype(f32) + d[...].astype(f32)).astype(bf16)


def pair_sums(a, b, c, d):
    return pl.pallas_call(
        pair_kernel,
        out_shape=(shape((1024, EMB), bf16),) * 2,
        in_specs=[VMEM] * 4,
        out_specs=[VMEM] * 2,
        compiler_params=params(16),
        name="pair_sums",
    )(a, b, c, d)


def cold_update_kernel(a, b, c, d, table_ref, accum_ref, new_ref, accum_new_ref):
    for block in range(16):
        one, two = (a, b) if block < 8 else (c, d)
        at = slice((block % 8) * 128, (block % 8) * 128 + 128)
        rows = slice(block * 128, block * 128 + 128)
        grad = one[at, :].astype(f32) + two[at, :].astype(f32)
        new_ref[rows, :], accum_new_ref[block : block + 1, :] = row_update(
            table_ref[rows, :], accum_ref[block : block + 1, :], grad
        )


def update_cold(a, b, c, d, table, accum):
    return pl.pallas_call(
        cold_update_kernel,
        out_shape=(shape((R_OWN, EMB), f32), shape((R_OWN // 128, 128), f32)),
        in_specs=[VMEM] * 6,
        out_specs=[VMEM] * 2,
        compiler_params=params(16),
        name="cold_update",
    )(a, b, c, d, table, accum)


def dp_index(z, x, core):
    return (z * 4 + x) * 2 + core


def over_core(value):
    pairs = [
        (dp_index(z, x, core), dp_index(z, x, 1 - core))
        for z in range(8)
        for x in range(4)
        for core in range(2)
    ]
    return lax.ppermute(value, "dp", pairs)


def over_axis(value, axis):
    swap = (lambda i: 3 - i) if axis in (0, 2) else (lambda i: i ^ 1)
    if axis >= 2:
        return lax.ppermute(value, "rep", [(y, swap(y)) for y in range(4)])
    pairs = [
        (dp_index(z, x, core), dp_index(z, swap(x), core))
        for z in range(8)
        for x in range(4)
        for core in range(2)
    ]
    return lax.ppermute(value, "dp", pairs)


def over_z(value):
    groups = [[dp_index(z, x, core) for z in range(8)] for x in range(4) for core in range(2)]
    return lax.all_to_all(
        value, "dp", split_axis=0, concat_axis=0, tiled=True, axis_index_groups=groups
    )


def on_device(
    hot_slab,
    hot_accum,
    cold_table,
    cold_accum,
    touched_owner,
    touched_row,
    lookup_index,
    bag_id,
    labels,
    w_hidden,
    hidden_accum,
    w_out,
    out_accum,
):
    dp = lax.axis_index("dp")
    y = lax.axis_index("rep")
    core, x = dp & 1, (dp >> 1) & 3
    position = dp * 4 + y
    bits = ((x ^ (x >> 1)) << 2) | (y ^ (y >> 1))
    mine = jnp.stack([(core << 9) | (bits << 5), core, bits]).astype(i32)

    rows = LOOK // 128
    look = lookup_index.reshape(rows, 128)
    spare = HOT + (lax.broadcasted_iota(i32, (rows, 128), 1) & (GROUP - 1))
    look = jnp.where(look < HOT, look, spare)
    look_flat = look.reshape(LOOK)
    bag_rows = bag_id.reshape(BLOCKS, BLOCK)
    first = bag_rows[:, 0]

    requests, pos, clash = route(
        touched_owner.reshape(1, UNIQ), touched_row.reshape(1, UNIQ), look
    )
    pos_flat = pos.reshape(UNIQ)
    counts = slot_counts(first, lookup_index.reshape(BLOCKS, BLOCK), bag_rows)
    asked = lax.all_to_all(requests, "dp", split_axis=0, concat_axis=0, tiled=True)
    asked, counts = lax.optimization_barrier((asked, counts))
    found = found_rows(jnp.maximum(asked, 0).reshape(SLOTS), cold_table)
    returned = lax.all_to_all(
        found.reshape(N_DP, CAP, EMB), "dp", split_axis=0, concat_axis=0, tiled=True
    ).reshape(SLOTS, EMB)
    pooled = pool_hot(first, look_flat, bag_rows, hot_slab)
    bag_grad, outgoing, factors, out_grad = layer(
        pos_flat,
        pooled,
        counts,
        returned,
        labels.reshape(B_DEV, 1),
        w_hidden,
        w_out.reshape(1, HID),
    )
    incoming = lax.all_to_all(
        outgoing.reshape(N_DP, CAP, EMB), "dp", split_axis=0, concat_axis=0, tiled=True
    ).reshape(SLOTS, EMB)
    other_factors = over_core(factors)
    out_grad = out_grad.reshape(8, EMB)
    out_recv = over_core(out_grad)
    clashes = jnp.max(clash.reshape(BLOCKS, BLOCK // GROUP), axis=1)
    keep, send = scatter_hot(
        look_flat, clash.reshape(LOOK // GROUP), clashes, first, mine, bag_rows, bag_grad
    )
    send, incoming = lax.optimization_barrier((send, incoming))
    recv = over_core(send)
    hidden = hidden_half(mine, factors, other_factors)
    cold_a, cold_b = cold_grads(asked.reshape(1, SLOTS), incoming)
    recv_a, recv_b = over_axis(cold_a, 3), over_axis(cold_b, 2)
    sends = first_send(keep, recv, hidden, out_grad, out_recv)
    recv_a, recv_b, *sends = lax.optimization_barrier((recv_a, recv_b, *sends))
    keeps = first_keep(keep, recv, hidden)
    for step in range(4):
        travelled = [over_axis(sends[s], ORDERS[s][step]) for s in range(4)] + [sends[4]]
        if step < 3:
            sends, keeps = next_step(step + 1, travelled, keeps)
    pair_a, pair_b = pair_sums(cold_a, recv_a, cold_b, recv_b)
    parts, pair_a, pair_b = lax.optimization_barrier((last_step(travelled, keeps), pair_a, pair_b))
    recv_a, recv_b = over_axis(pair_a, 2), over_axis(pair_b, 3)
    parts = over_z(parts)
    cold_new, cold_accum_new = update_cold(
        pair_a, recv_a, pair_b, recv_b, cold_table, cold_accum.reshape(R_OWN // 128, 128)
    )

    own_slab = lax.dynamic_slice_in_dim(hot_slab, position * 128, 128, 0)
    own_hidden = lax.dynamic_slice_in_dim(w_hidden, position * 4, 4, 0).astype(f32)
    own_out = lax.dynamic_slice_in_dim(w_out, position * 4, 4, 0)
    hot_new, hot_accum_new, hidden_new, hidden_accum_new, out_total = update_owned(
        parts, own_slab, hot_accum.reshape(1, 128), own_hidden, hidden_accum
    )
    out_part = lax.dynamic_slice_in_dim(out_total.reshape(HID), position * 4, 4, 0)
    out_accum_new = out_accum + out_part * out_part
    out_new = own_out - learn_rate * out_part / jnp.sqrt(out_accum_new)
    return (
        hot_new,
        hot_accum_new.reshape(128),
        cold_new,
        cold_accum_new.reshape(R_OWN),
        hidden_new,
        hidden_accum_new,
        out_new,
        out_accum_new,
    )


def solution(mesh):
    both = ("dp", "rep")
    in_specs = (
        P(),
        P(both),
        P("dp", None),
        P("dp"),
        P(both, None),
        P(both),
        P(both),
        P(both, None),
        P(both),
        P(),
        P(both, None),
        P(),
        P(both),
    )
    out_specs = (
        P(both, None),
        P(both),
        P("dp", None),
        P("dp"),
        P(both, None),
        P(both, None),
        P(both),
        P(both),
    )
    return jax.shard_map(
        on_device, mesh=mesh, in_specs=in_specs, out_specs=out_specs, check_vma=False
    )
```

time: 1990 us -> 224 us (0.11)
  waiting for transfers between devices: 1510 us -> 50.1 us
  other arithmetic: 288 us -> 3.88 us
  Pallas kernels: 0 us -> 80.2 us
  blocking collectives: 75.6 us -> 0 us
  starting transfers between devices: 23.7 us -> 65.9 us
  local copies, waits for them, and re-layouts: 52.8 us -> 21.8 us
    reduce_scatter x1 -> x0, waiting for transfers between devices: 1280 us -> none  [on_device(): lax.psum_scatter(dense_grad, ('dp', 'rep'), scatter_dimension=0, tiled=True)]
    scatter-add x4 -> x0, other arithmetic: 253 us -> none  [the longest x1 130 us: local_pass(): jax.ops.segment_sum(values, bag_ids, num_segments=bag_count, indices_are_...]
    psum x2 -> x0, waiting for transfers between devices: 178 us -> none  [the longest x1 178 us: on_device(): hidden_total, out_total = lax.psum((hidden_grad, out_grad), ('dp', 'rep'))]
    pallas_call x0 -> x17, Pallas kernels: none -> 80.2 us  [the longest x1 20.3 us: scatter_hot(): pl.pallas_call(scatter_kernel, out_shape=(shape((4, 16, 8, 32, EMB), f32)...]
    psum x1 -> x0, blocking collectives: 75.6 us -> none  [on_device(): hidden_total, out_total = lax.psum((hidden_grad, out_grad), ('dp', 'rep'))]
    gather x3 -> x0, local copies, waits for them, and re-layouts: 39.2 us -> none  [the longest x1 27.7 us: local_pass(): jnp.take(input_grad.reshape(bag_count, emb_width), bag_ids, axis=0)]
    ppermute x0 -> x23, waiting for transfers between devices: none -> 38.4 us  [the longest x12 30.7 us: over_axis(): return lax.ppermute(value, 'rep', [(y, swap(y)) for y in range(4)])]
    all_to_all x2 -> x3, waiting for transfers between devices: 46.2 us -> 11.8 us  [the longest x1 6.08 us: on_device(): lax.all_to_all(found.reshape(N_DP, CAP, EMB), 'dp', split_axis=0, concat_...]
  transfers between devices with their start and end apart: 6 -> 27, of which waited for: 5 -> 16; matrix products, arithmetic and copies ran while one was open for 3% -> 2% of each run, Pallas kernels for 0% -> 27%
where the time goes in v1:
time: 224 us; the launch traced here: 223 us
  Pallas kernels  80.2 us (36%)
  starting transfers between devices  65.9 us (29%)
  waiting for transfers between devices  50.1 us (22%)
  local copies, waits for them, and re-layouts  21.8 us (10%)
  other arithmetic  3.88 us (2%)
    ppermute x12, waiting for transfers between devices, over_axis(): return lax.ppermute(value, 'rep', [(y, swap(y)) for y in range(4)])  30.7 us
    pallas_call x1, Pallas kernels, scatter_hot(): pl.pallas_call(scatter_kernel, out_shape=(shape((4, 16, 8, 32, EMB), f32)...  20.3 us
    unnamed x45, local copies, waits for them, and re-layouts  19.6 us
    ppermute x12, starting transfers between devices, over_axis(): return lax.ppermute(value, 'rep', [(y, swap(y)) for y in range(4)])  17.3 us
    pallas_call x1, Pallas kernels, pool_hot(): pl.pallas_call(pool_kernel, out_shape=shape((BAGS, EMB), f32), in_specs=[...  13.5 us
    pallas_call x1, Pallas kernels, slot_counts(): pl.pallas_call(counts_kernel, out_shape=shape((BAGS, UNIQ), bf16), in_spe...  12.9 us
    ppermute x8, starting transfers between devices, over_axis(): return lax.ppermute(value, 'dp', pairs)  12 us
    all_to_all x1, starting transfers between devices, on_device(): lax.all_to_all(requests, 'dp', split_axis=0, concat_axis=0, tiled=True)  12 us
  transfers between devices with their start and end apart: 27, of which 16 were waited for; matrix products, arithmetic and copies ran while one was open for 2% of the time, Pallas kernels for 27%

profile of v1, /device:TPU:2, one launch (start us, length us, event | category | flops | bytes accessed | tf_op | source)
XLA Modules:
  0.0 222.9 jit_solution(13886869767197488218)
XLA Ops:
  4.0 12.0 %all-to-all-start = ((s32[64,1,48]{2,1,0:T(1,128)}), s32[64,1,48]{2,1,0:T(1,128)S(1)}, u32[]{:S(2)}, u32[]{:S(2)}) async-start(s32[64,1,48]{2,1,0:T(1,128)} %bitcast.4), calls=%async_computation | async-start | bytes 65536 | tf_op jit(solution)/shard_map/all_to_all | solution.py:832
  19.0 12.9 %counts.1.counts_ref = bf16[2048,1024]{1,0:T(8,128)(2,1)S(1)} custom-call(s32[32]{0:T(128)S(1)} %slice_reduce_fusion.first_ref, s32[32,256]{1,0:T(8,128)S(1)} %reshape.91.look_ref, s32[32,256]{1,0:T(8,128)S(1)} %reshape.90.bag_ref), custom_call_target="tpu_custom_call" | custom-call | flops 5000000000 | bytes 8388608 | tf_op jit(solution)/shard_map/counts/pallas_call | solution.py:145
  31.9 2.0 copy-done.15
  33.9 5.0 %found.1 = bf16[3072,128]{1,0:T(8,128)(2,1)} custom-call(s32[3072]{0:T(1024)S(1)} %reshape.95.asked_ref, f32[2048,128]{1,0:T(8,128)S(1)} %copy-done.2), custom_call_target="tpu_custom_call" | custom-call | tf_op jit(solution)/shard_map/found/pallas_call | solution.py:119
  38.9 10.3 %all-to-all-start.1 = ((bf16[64,48,128]{2,1,0:T(8,128)(2,1)}), bf16[64,48,128]{2,1,0:T(8,128)(2,1)S(1)}, u32[]{:S(2)}, u32[]{:S(2)}) async-start(bf16[64,48,128]{2,1,0:T(8,128)(2,1)} %bitcast.11), calls=%async_computation.1 | async-start | bytes 1572864 | tf_op jit(solution)/shard_map/all_to_all | solution.py:835
  49.4 3.4 %copy-done.1 = bf16[32768,128]{1,0:T(8,128)(2,1)S(1)} copy-done((bf16[32768,128]{1,0:T(8,128)(2,1)S(1)}, bf16[32768,128]{1,0:T(8,128)(2,1)}, u32[]{:S(2)}) %copy-start.1) | copy-done | bytes 8388632
  52.8 13.5 %pool.1.pooled_ref = f32[2048,128]{1,0:T(8,128)S(1)} custom-call(s32[32]{0:T(128)S(1)} %slice_reduce_fusion.first_ref, s32[8192]{0:T(1024)S(1)} %compare_select_fusion.look_ref, s32[32,256]{1,0:T(8,128)S(1)} %reshape.90.bag_ref, bf16[32768,128]{1,0:T(8,128)(2,1)S(1)} %copy-done.1), custom_call_target="tpu_custom_call" | custom-call | flops 1000000000 | bytes 41943040 | tf_op jit(solution)/shard_map/pool/pallas_call | solution.py:214
  66.3 6.1 %all-to-all-done.1 = bf16[64,48,128]{2,1,0:T(8,128)(2,1)S(1)} async-done(((bf16[64,48,128]{2,1,0:T(8,128)(2,1)}), bf16[64,48,128]{2,1,0:T(8,128)(2,1)S(1)}, u32[]{:S(2)}, u32[]{:S(2)}) %all-to-all-start.1) | async-done | bytes 786464 | tf_op jit(solution)/shard_map/all_to_all | solution.py:835
  74.0 2.2 copy-done.16
  76.2 10.3 %layer.1 = (f32[2048,128]{1,0:T(8,128)S(1)}, bf16[3072,128]{1,0:T(8,128)(2,1)}, bf16[2,256,1024]{2,1,0:T(8,128)(2,1)S(1)}, f32[1,1024]{1,0:T(1,128)S(1)}) custom-call(s32[1024]{0:T(1024)S(1)} %bitcast.38, f32[2048,128]{1,0:T(8,128)S(1)} %pool.1.pooled_ref, bf16[2048,1024]{1,0:T(8,128)(2,1)S(1)} %copy-done.16, bf16[3072,128]{1,0:T(8,128)(2,1)S(1)} %bitcast.29, ...), custom_call_target="tpu_custom_call" | custom-call | flops 4000000000 | bytes 20971520 | tf_op jit(solution)/shard_map/layer/pallas_call | solution.py:294
  88.5 5.9 %all-to-all-start.2 = ((bf16[64,48,128]{2,1,0:T(8,128)(2,1)}), bf16[64,48,128]{2,1,0:T(8,128)(2,1)S(1)}, u32[]{:S(2)}, u32[]{:S(2)}) async-start(bf16[64,48,128]{2,1,0:T(8,128)(2,1)} %bitcast.15), calls=%async_computation.2 | async-start | bytes 1572864 | tf_op jit(solution)/shard_map/all_to_all | solution.py:848
  96.2 20.3 %scatter.1 = (f32[4,16,8,32,128]{4,3,2,1,0:T(8,128)S(1)}, bf16[4,16,8,32,128]{4,3,2,1,0:T(8,128)(2,1)S(1)}) custom-call(s32[8192]{0:T(1024)S(1)} %compare_select_fusion.look_ref, s32[512]{0:T(512)S(1)} %reshape.93.clash_ref, s32[32]{0:T(128)S(1)} %reduce_max.18.clashes_ref, s32[32]{0:T(128)S(1)} %slice_reduce_fusion.first_ref, s32[3]{0:T(128)S(1)} %pad_add_fusion.mine_ref, ...), custom_call_target="tpu_custom_call" | custom-call | flops 1000000000 | bytes 83886080 | tf_op jit(solution)/shard_map/scatter/pallas_call | solution.py:422
  116.5 3.3 %copy-done = f32[4,16,8,32,128]{4,3,2,1,0:T(8,128)} copy-done((f32[4,16,8,32,128]{4,3,2,1,0:T(8,128)}, f32[4,16,8,32,128]{4,3,2,1,0:T(8,128)S(1)}, u32[]{:S(2)}) %copy-start) | copy-done | bytes 8388632
  119.8 2.1 copy-done.10
  124.0 3.4 %cold_grads.1 = (bf16[1024,128]{1,0:T(8,128)(2,1)S(1)}, bf16[1024,128]{1,0:T(8,128)(2,1)S(1)}) custom-call(s32[1,3072]{1,0:T(1,128)S(1)} %reshape.92.asked_ref, bf16[3072,128]{1,0:T(8,128)(2,1)S(1)} %bitcast.28), custom_call_target="tpu_custom_call" | custom-call | flops 2000000000 | bytes 4194304 | tf_op jit(solution)/shard_map/cold_grads/pallas_call | solution.py:714
  127.6 3.7 %collective-permute-start.1 = (bf16[1024,128]{1,0:T(8,128)(2,1)S(1)}, bf16[1024,128]{1,0:T(8,128)(2,1)S(1)}, u32[]{:S(2)}, u32[]{:S(2)}) collective-permute-start(bf16[1024,128]{1,0:T(8,128)(2,1)S(1)} %get-tuple-element.104.c), channel_id=1, source_target_pairs={{0,3},{1,2},{2,1},{3,0},{4,7},{5,6},{6,5},{7,4},{8,11},{9,10},{10,... | collective-permute-start | bytes 786440 | tf_op jit(solution)/shard_map/ppermute | solution.py:780
  131.6 2.8 %hidden_half.1.hidden_ref = f32[512,1024]{1,0:T(8,128)S(1)} custom-call(s32[3]{0:T(128)S(1)} %pad_add_fusion.mine_ref, bf16[2,256,1024]{2,1,0:T(8,128)(2,1)S(1)} %copy-done.12, bf16[2,256,1024]{2,1,0:T(8,128)(2,1)} %collective-permute-done.3.two_ref), custom_call_target="tpu_custom_call" | custom-call | flops 4000000000 | bytes 4194304 | tf_op jit(solution)/shard_map/hidden_half/pallas_call | solution.py:323
  134.4 2.9 %first_send.1 = (bf16[3088,128]{1,0:T(8,128)(2,1)S(1)}, bf16[3072,128]{1,0:T(8,128)(2,1)S(1)}, bf16[3072,128]{1,0:T(8,128)(2,1)S(1)}, bf16[3072,128]{1,0:T(8,128)(2,1)S(1)}, f32[8,128]{1,0:T(8,128)S(1)}) custom-call(f32[4,16,8,32,128]{4,3,2,1,0:T(8,128)S(1)} %bitcast.27, bf16[4,16,8,32,128]{4,3,2,1,0:T(8,128)(2,1)} %collective-permute-done.2.recv_ref, ...), custom_call_target="tpu_custom_call" | custom-call | flops 1000000 | bytes 12582912 | tf_op jit(solution)/shard_map/first_send/pallas_call | solution.py:546
  138.3 2.5 %collective-permute-start.6 = (bf16[3072,128]{1,0:T(8,128)(2,1)S(1)}, bf16[3072,128]{1,0:T(8,128)(2,1)S(1)}, u32[]{:S(2)}, u32[]{:S(2)}) collective-permute-start(bf16[3072,128]{1,0:T(8,128)(2,1)S(1)} %get-tuple-element.115), channel_id=1, source_target_pairs={{0,3},{1,2},{2,1},{3,0},{4,7},{5,6},{6,5},{7,4},{8,11},{9,10},{10,... | collective-permute-start | bytes 2359304 | tf_op jit(solution)/shard_map/ppermute | solution.py:780
  142.2 2.0 collective-permute-start.8
  144.2 2.8 %first_keep.1 = (f32[8,8,32,128]{3,2,1,0:T(8,128)S(1)}, f32[8,8,32,128]{3,2,1,0:T(8,128)S(1)}, f32[8,8,32,128]{3,2,1,0:T(8,128)S(1)}, f32[8,8,32,128]{3,2,1,0:T(...) custom-call(f32[4,16,8,32,128]{4,3,2,1,0:T(8,128)S(1)} %bitcast.27, ...), custom_call_target="tpu_custom_call" | custom-call | flops 1000000 | bytes 12582912 | tf_op jit(solution)/shard_map/first_keep/pallas_call | solution.py:572
  147.0 11.5 %collective-permute-done.6.refs_1_ = bf16[3072,128]{1,0:T(8,128)(2,1)S(1)} collective-permute-done((bf16[3072,128]{1,0:T(8,128)(2,1)S(1)}, bf16[3072,128]{1,0:T(8,128)(2,1)S(1)}, u32[]{:S(2)}, u32[]{:S(2)}) %collective-permute-start.6) | collective-permute-done | bytes 786464 | tf_op jit(solution)/shard_map/ppermute | solution.py:780
  161.7 2.3 %collective-permute-start.9 = (bf16[1552,128]{1,0:T(8,128)(2,1)S(1)}, bf16[1552,128]{1,0:T(8,128)(2,1)S(1)}, u32[]{:S(2)}, u32[]{:S(2)}) collective-permute-start(bf16[1552,128]{1,0:T(8,128)(2,1)S(1)} %get-tuple-element.127), channel_id=1, source_target_pairs={{0,3},{1,2},{2,1},{3,0},{4,7},{5,6},{6,5},{7,4},{8,11},{9,10},{10,... | collective-permute-start | bytes 1191944 | tf_op jit(solution)/shard_map/ppermute | solution.py:780
  164.9 2.3 %collective-permute-start.12 = (bf16[1536,128]{1,0:T(8,128)(2,1)S(1)}, bf16[1536,128]{1,0:T(8,128)(2,1)S(1)}, u32[]{:S(2)}, u32[]{:S(2)}) collective-permute-start(bf16[1536,128]{1,0:T(8,128)(2,1)S(1)} %get-tuple-element.130), channel_id=1, source_target_pairs={{0,8},{4,12},{8,0},{12,4},{16,24},{20,28},{24,16},{28,20},{32,40},... | collective-permute-start | bytes 1179656 | tf_op jit(solution)/shard_map/ppermute | solution.py:787
  167.2 5.9 %collective-permute-done.10.refs_1_ = bf16[1536,128]{1,0:T(8,128)(2,1)S(1)} collective-permute-done((bf16[1536,128]{1,0:T(8,128)(2,1)S(1)}, bf16[1536,128]{1,0:T(8,128)(2,1)S(1)}, u32[]{:S(2)}, u32[]{:S(2)}) %collective-permute-start.10) | collective-permute-done | bytes 393248 | tf_op jit(solution)/shard_map/ppermute | solution.py:780
  179.7 2.6 %collective-permute-start.16 = (bf16[1280,128]{1,0:T(8,128)(2,1)S(1)}, bf16[1280,128]{1,0:T(8,128)(2,1)S(1)}, u32[]{:S(2)}, u32[]{:S(2)}) collective-permute-start(bf16[1280,128]{1,0:T(8,128)(2,1)S(1)} %get-tuple-element.143), channel_id=1, source_target_pairs={{0,3},{1,2},{2,1},{3,0},{4,7},{5,6},{6,5},{7,4},{8,11},{9,10},{10,... | collective-permute-start | bytes 983048 | tf_op jit(solution)/shard_map/ppermute | solution.py:780
  185.1 3.0 %collective-permute-done.16.refs_3_ = bf16[1280,128]{1,0:T(8,128)(2,1)S(1)} collective-permute-done((bf16[1280,128]{1,0:T(8,128)(2,1)S(1)}, bf16[1280,128]{1,0:T(8,128)(2,1)S(1)}, u32[]{:S(2)}, u32[]{:S(2)}) %collective-permute-start.16) | collective-permute-done | bytes 327712 | tf_op jit(solution)/shard_map/ppermute | solution.py:780
  191.0 2.6 %collective-permute-start.19 = (bf16[640,128]{1,0:T(8,128)(2,1)S(1)}, bf16[640,128]{1,0:T(8,128)(2,1)S(1)}, u32[]{:S(2)}, u32[]{:S(2)}) collective-permute-start(bf16[640,128]{1,0:T(8,128)(2,1)S(1)} %get-tuple-element.155), channel_id=1, source_target_pairs={{0,3},{1,2},{2,1},{3,0},{4,7},{5,6},{6,5},{7,4},{8,11},{9,10},{10,... | collective-permute-start | bytes 491528 | tf_op jit(solution)/shard_map/ppermute | solution.py:780
  194.8 2.7 %collective-permute-done.19.refs_2_ = bf16[640,128]{1,0:T(8,128)(2,1)S(1)} collective-permute-done((bf16[640,128]{1,0:T(8,128)(2,1)S(1)}, bf16[640,128]{1,0:T(8,128)(2,1)S(1)}, u32[]{:S(2)}, u32[]{:S(2)}) %collective-permute-start.19) | collective-permute-done | bytes 163872 | tf_op jit(solution)/shard_map/ppermute | solution.py:780
  200.0 6.3 %all-to-all-start.3 = ((bf16[8,336,128]{2,1,0:T(8,128)(2,1)}), bf16[8,336,128]{2,1,0:T(8,128)(2,1)S(1)}, u32[]{:S(2)}, u32[]{:S(2)}) async-start(bf16[8,336,128]{2,1,0:T(8,128)(2,1)} %step_5.1), calls=%async_computation.3 | async-start | bytes 1376256 | tf_op jit(solution)/shard_map/all_to_all | solution.py:792
  209.0 4.9 %collective-permute-done.21.b = bf16[1024,128]{1,0:T(8,128)(2,1)S(1)} collective-permute-done((bf16[1024,128]{1,0:T(8,128)(2,1)S(1)}, bf16[1024,128]{1,0:T(8,128)(2,1)S(1)}, u32[]{:S(2)}, u32[]{:S(2)}) %collective-permute-start.21) | collective-permute-done | bytes 262176 | tf_op jit(solution)/shard_map/ppermute | solution.py:780
  215.7 5.7 %all-to-all-done.3.recv_ref = bf16[8,336,128]{2,1,0:T(8,128)(2,1)S(1)} async-done(((bf16[8,336,128]{2,1,0:T(8,128)(2,1)}), bf16[8,336,128]{2,1,0:T(8,128)(2,1)S(1)}, u32[]{:S(2)}, u32[]{:S(2)}) %all-to-all-start.3) | async-done | bytes 688160 | tf_op jit(solution)/shard_map/all_to_all | solution.py:792
  (104 shorter events, 42.7 us)
Async XLA Ops:
  4.0 29.8 %all-to-all-start = ((s32[64,1,48]{2,1,0:T(1,128)}), s32[64,1,48]{2,1,0:T(1,128)S(1)}, u32[]{:S(2)}, u32[]{:S(2)}) async-start(s32[64,1,48]{2,1,0:T(1,128)} %bitcast.4), calls=%async_computation | async-start | bytes 65536 | tf_op jit(solution)/shard_map/all_to_all | solution.py:832
  38.9 33.5 %all-to-all-start.1 = ((bf16[64,48,128]{2,1,0:T(8,128)(2,1)}), bf16[64,48,128]{2,1,0:T(8,128)(2,1)S(1)}, u32[]{:S(2)}, u32[]{:S(2)}) async-start(bf16[64,48,128]{2,1,0:T(8,128)(2,1)} %bitcast.11), calls=%async_computation.1 | async-start | bytes 1572864 | tf_op jit(solution)/shard_map/all_to_all | solution.py:835
  88.5 34.8 %copy-start.12 = (bf16[2,256,1024]{2,1,0:T(8,128)(2,1)S(1)}, bf16[2,256,1024]{2,1,0:T(8,128)(2,1)}, u32[]{:S(2)}) copy-start(bf16[2,256,1024]{2,1,0:T(8,128)(2,1)} %copy-done.11) | copy-start | bytes 3145732
  88.5 33.4 %all-to-all-start.2 = ((bf16[64,48,128]{2,1,0:T(8,128)(2,1)}), bf16[64,48,128]{2,1,0:T(8,128)(2,1)S(1)}, u32[]{:S(2)}, u32[]{:S(2)}) async-start(bf16[64,48,128]{2,1,0:T(8,128)(2,1)} %bitcast.15), calls=%async_computation.2 | async-start | bytes 1572864 | tf_op jit(solution)/shard_map/all_to_all | solution.py:848
  121.9 12.5 %collective-permute-start.2 = (bf16[4,16,8,32,128]{4,3,2,1,0:T(8,128)(2,1)}, bf16[4,16,8,32,128]{4,3,2,1,0:T(8,128)(2,1)}, u32[]{:S(2)}, u32[]{:S(2)}) collective-permute-start(bf16[4,16,8,32,128]{4,3,2,1,0:T(8,128)(2,1)} %copy-done.10), channel_id=1, source_target_pairs={{0,4},{4,0},{8,12},{12,8},{16,20},{20,16},{24,28},{28,24},{32,36},... | collective-permute-start | bytes 12582920 | tf_op jit(solution)/shard_map/ppermute | solution.py:774
  123.3 8.3 %collective-permute-start.3 = (bf16[2,256,1024]{2,1,0:T(8,128)(2,1)S(1)}, bf16[2,256,1024]{2,1,0:T(8,128)(2,1)}, u32[]{:S(2)}, u32[]{:S(2)}) collective-permute-start(bf16[2,256,1024]{2,1,0:T(8,128)(2,1)S(1)} %copy-done.12), channel_id=1, source_target_pairs={{0,4},{4,0},{8,12},{12,8},{16,20},{20,16},{24,28},{28,24},{32,36},... | collective-permute-start | bytes 3145736 | tf_op jit(solution)/shard_map/ppermute | solution.py:774
  123.5 10.9 %collective-permute-start.4 = (f32[8,128]{1,0:T(8,128)S(1)}, f32[8,128]{1,0:T(8,128)S(1)}, u32[]{:S(2)}, u32[]{:S(2)}) collective-permute-start(f32[8,128]{1,0:T(8,128)S(1)} %bitcast.31), channel_id=1, source_target_pairs={{0,4},{4,0},{8,12},{12,8},{16,20},{20,16},{24,28},{28,24},{32,36},... | collective-permute-start | bytes 12296 | tf_op jit(solution)/shard_map/ppermute | solution.py:774
  127.4 9.9 %collective-permute-start = (bf16[1024,128]{1,0:T(8,128)(2,1)S(1)}, bf16[1024,128]{1,0:T(8,128)(2,1)S(1)}, u32[]{:S(2)}, u32[]{:S(2)}) collective-permute-start(bf16[1024,128]{1,0:T(8,128)(2,1)S(1)} %get-tuple-element.103.a), channel_id=1, source_target_pairs={{0,1},{1,0},{2,3},{3,2},{4,5},{5,4},{6,7},{7,6},{8,9},{9,8},{10,11... | collective-permute-start | bytes 786440 | tf_op jit(solution)/shard_map/ppermute | solution.py:780
  127.6 10.3 %collective-permute-start.1 = (bf16[1024,128]{1,0:T(8,128)(2,1)S(1)}, bf16[1024,128]{1,0:T(8,128)(2,1)S(1)}, u32[]{:S(2)}, u32[]{:S(2)}) collective-permute-start(bf16[1024,128]{1,0:T(8,128)(2,1)S(1)} %get-tuple-element.104.c), channel_id=1, source_target_pairs={{0,3},{1,2},{2,1},{3,0},{4,7},{5,6},{6,5},{7,4},{8,11},{9,10},{10,... | collective-permute-start | bytes 786440 | tf_op jit(solution)/shard_map/ppermute | solution.py:780
  137.8 23.3 %collective-permute-start.5 = (bf16[3088,128]{1,0:T(8,128)(2,1)S(1)}, bf16[3088,128]{1,0:T(8,128)(2,1)S(1)}, u32[]{:S(2)}, u32[]{:S(2)}) collective-permute-start(bf16[3088,128]{1,0:T(8,128)(2,1)S(1)} %get-tuple-element.114), channel_id=1, source_target_pairs={{0,1},{1,0},{2,3},{3,2},{4,5},{5,4},{6,7},{7,6},{8,9},{9,8},{10,11... | collective-permute-start | bytes 2371592 | tf_op jit(solution)/shard_map/ppermute | solution.py:780
  138.3 20.2 %collective-permute-start.6 = (bf16[3072,128]{1,0:T(8,128)(2,1)S(1)}, bf16[3072,128]{1,0:T(8,128)(2,1)S(1)}, u32[]{:S(2)}, u32[]{:S(2)}) collective-permute-start(bf16[3072,128]{1,0:T(8,128)(2,1)S(1)} %get-tuple-element.115), channel_id=1, source_target_pairs={{0,3},{1,2},{2,1},{3,0},{4,7},{5,6},{6,5},{7,4},{8,11},{9,10},{10,... | collective-permute-start | bytes 2359304 | tf_op jit(solution)/shard_map/ppermute | solution.py:780
  140.8 19.1 %collective-permute-start.7 = (bf16[3072,128]{1,0:T(8,128)(2,1)S(1)}, bf16[3072,128]{1,0:T(8,128)(2,1)S(1)}, u32[]{:S(2)}, u32[]{:S(2)}) collective-permute-start(bf16[3072,128]{1,0:T(8,128)(2,1)S(1)} %get-tuple-element.116), channel_id=1, source_target_pairs={{0,8},{4,12},{8,0},{12,4},{16,24},{20,28},{24,16},{28,20},{32,40},... | collective-permute-start | bytes 2359304 | tf_op jit(solution)/shard_map/ppermute | solution.py:787
  142.2 19.0 %collective-permute-start.8 = (bf16[3072,128]{1,0:T(8,128)(2,1)S(1)}, bf16[3072,128]{1,0:T(8,128)(2,1)S(1)}, u32[]{:S(2)}, u32[]{:S(2)}) collective-permute-start(bf16[3072,128]{1,0:T(8,128)(2,1)S(1)} %get-tuple-element.117), channel_id=1, source_target_pairs={{0,24},{4,28},{8,16},{12,20},{16,8},{20,12},{24,0},{28,4},{32,56},... | collective-permute-start | bytes 2359304 | tf_op jit(solution)/shard_map/ppermute | solution.py:787
  161.7 13.1 %collective-permute-start.9 = (bf16[1552,128]{1,0:T(8,128)(2,1)S(1)}, bf16[1552,128]{1,0:T(8,128)(2,1)S(1)}, u32[]{:S(2)}, u32[]{:S(2)}) collective-permute-start(bf16[1552,128]{1,0:T(8,128)(2,1)S(1)} %get-tuple-element.127), channel_id=1, source_target_pairs={{0,3},{1,2},{2,1},{3,0},{4,7},{5,6},{6,5},{7,4},{8,11},{9,10},{10,... | collective-permute-start | bytes 1191944 | tf_op jit(solution)/shard_map/ppermute | solution.py:780
  164.0 9.1 %collective-permute-start.10 = (bf16[1536,128]{1,0:T(8,128)(2,1)S(1)}, bf16[1536,128]{1,0:T(8,128)(2,1)S(1)}, u32[]{:S(2)}, u32[]{:S(2)}) collective-permute-start(bf16[1536,128]{1,0:T(8,128)(2,1)S(1)} %get-tuple-element.128), channel_id=1, source_target_pairs={{0,1},{1,0},{2,3},{3,2},{4,5},{5,4},{6,7},{7,6},{8,9},{9,8},{10,11... | collective-permute-start | bytes 1179656 | tf_op jit(solution)/shard_map/ppermute | solution.py:780
  164.0 9.1 %collective-permute-start.11 = (bf16[1536,128]{1,0:T(8,128)(2,1)S(1)}, bf16[1536,128]{1,0:T(8,128)(2,1)S(1)}, u32[]{:S(2)}, u32[]{:S(2)}) collective-permute-start(bf16[1536,128]{1,0:T(8,128)(2,1)S(1)} %get-tuple-element.129), channel_id=1, source_target_pairs={{0,24},{4,28},{8,16},{12,20},{16,8},{20,12},{24,0},{28,4},{32,56},... | collective-permute-start | bytes 1179656 | tf_op jit(solution)/shard_map/ppermute | solution.py:787
  164.9 10.0 %collective-permute-start.12 = (bf16[1536,128]{1,0:T(8,128)(2,1)S(1)}, bf16[1536,128]{1,0:T(8,128)(2,1)S(1)}, u32[]{:S(2)}, u32[]{:S(2)}) collective-permute-start(bf16[1536,128]{1,0:T(8,128)(2,1)S(1)} %get-tuple-element.130), channel_id=1, source_target_pairs={{0,8},{4,12},{8,0},{12,4},{16,24},{20,28},{24,16},{28,20},{32,40},... | collective-permute-start | bytes 1179656 | tf_op jit(solution)/shard_map/ppermute | solution.py:787
  175.2 38.7 %copy-start.4 = (f32[2048]{0:T(1024)S(1)}, f32[2048]{0:T(1024)}, u32[]{:S(2)}) copy-start(f32[2048]{0:T(1024)} %param.16) | copy-start | bytes 24580
  175.3 12.8 %collective-permute-start.13 = (bf16[1296,128]{1,0:T(8,128)(2,1)S(1)}, bf16[1296,128]{1,0:T(8,128)(2,1)S(1)}, u32[]{:S(2)}, u32[]{:S(2)}) collective-permute-start(bf16[1296,128]{1,0:T(8,128)(2,1)S(1)} %get-tuple-element.140), channel_id=1, source_target_pairs={{0,8},{4,12},{8,0},{12,4},{16,24},{20,28},{24,16},{28,20},{32,40},... | collective-permute-start | bytes 995336 | tf_op jit(solution)/shard_map/ppermute | solution.py:787
  177.1 7.1 %collective-permute-start.14 = (bf16[1280,128]{1,0:T(8,128)(2,1)S(1)}, bf16[1280,128]{1,0:T(8,128)(2,1)S(1)}, u32[]{:S(2)}, u32[]{:S(2)}) collective-permute-start(bf16[1280,128]{1,0:T(8,128)(2,1)S(1)} %get-tuple-element.141), channel_id=1, source_target_pairs={{0,24},{4,28},{8,16},{12,20},{16,8},{20,12},{24,0},{28,4},{32,56},... | collective-permute-start | bytes 983048 | tf_op jit(solution)/shard_map/ppermute | solution.py:787
  178.0 7.1 %collective-permute-start.15 = (bf16[1280,128]{1,0:T(8,128)(2,1)S(1)}, bf16[1280,128]{1,0:T(8,128)(2,1)S(1)}, u32[]{:S(2)}, u32[]{:S(2)}) collective-permute-start(bf16[1280,128]{1,0:T(8,128)(2,1)S(1)} %get-tuple-element.142), channel_id=1, source_target_pairs={{0,1},{1,0},{2,3},{3,2},{4,5},{5,4},{6,7},{7,6},{8,9},{9,8},{10,11... | collective-permute-start | bytes 983048 | tf_op jit(solution)/shard_map/ppermute | solution.py:780
  179.7 8.3 %collective-permute-start.16 = (bf16[1280,128]{1,0:T(8,128)(2,1)S(1)}, bf16[1280,128]{1,0:T(8,128)(2,1)S(1)}, u32[]{:S(2)}, u32[]{:S(2)}) collective-permute-start(bf16[1280,128]{1,0:T(8,128)(2,1)S(1)} %get-tuple-element.143), channel_id=1, source_target_pairs={{0,3},{1,2},{2,1},{3,0},{4,7},{5,6},{6,5},{7,4},{8,11},{9,10},{10,... | collective-permute-start | bytes 983048 | tf_op jit(solution)/shard_map/ppermute | solution.py:780
  188.0 33.4 %copy-start.3 = (f32[4,1024]{1,0:T(4,128)S(1)}, f32[4,1024]{1,0:T(4,128)}, u32[]{:S(2)}) copy-start(f32[4,1024]{1,0:T(4,128)} %hid_accum_ref.1) | copy-start | bytes 49156
  188.0 33.4 %copy-start.7 = (f32[128]{0:T(128)S(1)}, f32[128]{0:T(128)}, u32[]{:S(2)}) copy-start(f32[128]{0:T(128)} %param.14) | copy-start | bytes 1540
  188.3 34.0 %copy-start.19 = (f32[4]{0:T(128)S(1)}, f32[4]{0:T(128)}, u32[]{:S(2)}) copy-start(f32[4]{0:T(128)} %param.25) | copy-start | bytes 52
  188.3 10.7 %collective-permute-start.17 = (bf16[656,128]{1,0:T(8,128)(2,1)S(1)}, bf16[656,128]{1,0:T(8,128)(2,1)S(1)}, u32[]{:S(2)}, u32[]{:S(2)}) collective-permute-start(bf16[656,128]{1,0:T(8,128)(2,1)S(1)} %get-tuple-element.153), channel_id=1, source_target_pairs={{0,24},{4,28},{8,16},{12,20},{16,8},{20,12},{24,0},{28,4},{32,56},... | collective-permute-start | bytes 503816 | tf_op jit(solution)/shard_map/ppermute | solution.py:787
  189.5 5.3 %collective-permute-start.18 = (bf16[640,128]{1,0:T(8,128)(2,1)S(1)}, bf16[640,128]{1,0:T(8,128)(2,1)S(1)}, u32[]{:S(2)}, u32[]{:S(2)}) collective-permute-start(bf16[640,128]{1,0:T(8,128)(2,1)S(1)} %get-tuple-element.154), channel_id=1, source_target_pairs={{0,8},{4,12},{8,0},{12,4},{16,24},{20,28},{24,16},{28,20},{32,40},... | collective-permute-start | bytes 491528 | tf_op jit(solution)/shard_map/ppermute | solution.py:787
  191.0 6.5 %collective-permute-start.19 = (bf16[640,128]{1,0:T(8,128)(2,1)S(1)}, bf16[640,128]{1,0:T(8,128)(2,1)S(1)}, u32[]{:S(2)}, u32[]{:S(2)}) collective-permute-start(bf16[640,128]{1,0:T(8,128)(2,1)S(1)} %get-tuple-element.155), channel_id=1, source_target_pairs={{0,3},{1,2},{2,1},{3,0},{4,7},{5,6},{6,5},{7,4},{8,11},{9,10},{10,... | collective-permute-start | bytes 491528 | tf_op jit(solution)/shard_map/ppermute | solution.py:780
  193.6 5.3 %collective-permute-start.20 = (bf16[640,128]{1,0:T(8,128)(2,1)S(1)}, bf16[640,128]{1,0:T(8,128)(2,1)S(1)}, u32[]{:S(2)}, u32[]{:S(2)}) collective-permute-start(bf16[640,128]{1,0:T(8,128)(2,1)S(1)} %get-tuple-element.156), channel_id=1, source_target_pairs={{0,1},{1,0},{2,3},{3,2},{4,5},{5,4},{6,7},{7,6},{8,9},{9,8},{10,11... | collective-permute-start | bytes 491528 | tf_op jit(solution)/shard_map/ppermute | solution.py:780
  200.0 21.4 %all-to-all-start.3 = ((bf16[8,336,128]{2,1,0:T(8,128)(2,1)}), bf16[8,336,128]{2,1,0:T(8,128)(2,1)S(1)}, u32[]{:S(2)}, u32[]{:S(2)}) async-start(bf16[8,336,128]{2,1,0:T(8,128)(2,1)} %step_5.1), calls=%async_computation.3 | async-start | bytes 1376256 | tf_op jit(solution)/shard_map/all_to_all | solution.py:792
  206.3 7.6 %collective-permute-start.21 = (bf16[1024,128]{1,0:T(8,128)(2,1)S(1)}, bf16[1024,128]{1,0:T(8,128)(2,1)S(1)}, u32[]{:S(2)}, u32[]{:S(2)}) collective-permute-start(bf16[1024,128]{1,0:T(8,128)(2,1)S(1)} %get-tuple-element.173.a), channel_id=1, source_target_pairs={{0,3},{1,2},{2,1},{3,0},{4,7},{5,6},{6,5},{7,4},{8,11},{9,10},{10,... | collective-permute-start | bytes 786440 | tf_op jit(solution)/shard_map/ppermute | solution.py:780
  207.5 6.4 %collective-permute-start.22 = (bf16[1024,128]{1,0:T(8,128)(2,1)S(1)}, bf16[1024,128]{1,0:T(8,128)(2,1)S(1)}, u32[]{:S(2)}, u32[]{:S(2)}) collective-permute-start(bf16[1024,128]{1,0:T(8,128)(2,1)S(1)} %get-tuple-element.174.c), channel_id=1, source_target_pairs={{0,1},{1,0},{2,3},{3,2},{4,5},{5,4},{6,7},{7,6},{8,9},{9,8},{10,11... | collective-permute-start | bytes 786440 | tf_op jit(solution)/shard_map/ppermute | solution.py:780
  (17 other events, 131.7 us)

commit v2 on v1

--- a/solution.py
+++ b/solution.py
@@ -27,7 +27,9 @@
 WINDOW = BLOCK + 16
 BLOCKS = LOOK // BLOCK
 BATCH = 4
-PADDED = BAGS + WINDOW
+FLAGS = 128
+ANY = FLAGS - 1
+LAST_START = BAGS - WINDOW
 MIB = 1 << 20
 
 ORDERS = ((3, 2, 1, 0), (2, 3, 0, 1), (1, 0, 3, 2), (0, 1, 2, 3))
@@ -61,9 +63,9 @@
     return lax.dot_general(a, b, (((0,), (0,)), ((), ())), preferred_element_type=f32)
 
 
-def route_kernel(owner_ref, row_ref, look_ref, request_ref, pos_ref, clash_ref):
+def route_kernel(owner_ref, row_ref, request_ref, pos_ref):
     owner = owner_ref[...]
-    row = row_ref[...] + 1
+    row = row_ref[...]
     member = lax.broadcasted_iota(i32, (N_DP, UNIQ), 0) == owner
     ones = member.astype(f32).astype(bf16)
     upper = lax.broadcasted_iota(i32, (UNIQ, UNIQ), 0) < lax.broadcasted_iota(
@@ -76,42 +78,54 @@
     high = jnp.where(member, (row >> 6).astype(f32), 0.0).astype(bf16)
     low = jnp.where(member, (row & 63).astype(f32), 0.0).astype(bf16)
     total = mm_nt(high, place) * 64.0 + mm_nt(low, place)
-    request_ref[...] = total.astype(i32) - 1
-    look = look_ref[...]
+    request_ref[...] = total.astype(i32)
+
+
+def route(owner, row):
+    return pl.pallas_call(
+        route_kernel,
+        out_shape=(shape((N_DP, CAP), i32), shape((1, UNIQ), i32)),
+        in_specs=[VMEM] * 2,
+        out_specs=[VMEM] * 2,
+        compiler_params=params(16),
+        name="route",
+    )(owner, row)
+
+
+def clash_kernel(look_ref, hot_ref, clash_ref):
     rows = LOOK // 128
     lane = lax.broadcasted_iota(i32, (rows, 128), 1) & (GROUP - 1)
+    look = look_ref[...]
+    look = jnp.where(look < HOT, look, HOT + lane)
+    hot_ref[...] = look
     clash = jnp.zeros((rows, 128), f32)
     for shift in range(1, GROUP):
         same = (look == pltpu.roll(look, shift, 1)) & (lane >= shift)
         clash = jnp.maximum(clash, same.astype(f32))
-    group = lax.broadcasted_iota(i32, (128, 128 // GROUP), 0) // GROUP
-    gather = group == lax.broadcasted_iota(i32, (128, 128 // GROUP), 1)
+    group = lax.broadcasted_iota(i32, (128, FLAGS), 0) // GROUP
+    column = lax.broadcasted_iota(i32, (128, FLAGS), 1)
+    gather = (group == column) | (column == ANY)
     clash_ref[...] = mm(clash.astype(bf16), gather.astype(f32).astype(bf16)).astype(i32)
 
 
-def route(owner, row, look):
-    return pl.pallas_call(
-        route_kernel,
-        out_shape=(
-            shape((N_DP, CAP), i32),
-            shape((1, UNIQ), i32),
-            shape((LOOK // 128, 128 // GROUP), i32),
-        ),
-        in_specs=[VMEM] * 3,
-        out_specs=[VMEM] * 3,
+def clashes(look):
+    return pl.pallas_call(
+        clash_kernel,
+        out_shape=(shape((LOOK // 128, 128), i32), shape((LOOK // 128, FLAGS), i32)),
+        in_specs=[VMEM],
+        out_specs=[VMEM] * 2,
         compiler_params=params(16),
-        name="route",
-    )(owner, row, look)
+        name="clashes",
+    )(look)
 
 
 def found_kernel(asked_ref, table_ref, found_ref, rows_ref):
-    def body(k, _):
-        for j in range(16):
-            at = k * 16 + j
-            rows_ref[pl.ds(at, 1), :] = table_ref[pl.ds(asked_ref[at], 1), :]
+    def body(owner, _):
+        for j in range(CAP):
+            rows_ref[pl.ds(owner * CAP + j, 1), :] = table_ref[pl.ds(asked_ref[owner, j], 1), :]
         return 0
 
-    lax.fori_loop(0, SLOTS // 16, body, 0)
+    lax.fori_loop(0, N_DP, body, 0)
     found_ref[...] = rows_ref[...].astype(bf16)
 
 
@@ -127,45 +141,90 @@
     )(asked, table)
 
 
-def counts_kernel(first_ref, look_ref, bag_ref, counts_ref, acc_ref):
+def one_hot(height, middle, numbers):
+    place = (lax.broadcasted_iota(i32, (height, 128), 0) - middle).astype(f32).astype(bf16)
+    inside = (numbers >= 0) & (numbers < height)
+    named = jnp.where(inside, numbers - middle, -middle - 2).astype(f32).astype(bf16)
+    return jnp.where(place == named, jnp.ones((), bf16), jnp.zeros((), bf16))
+
+
+def bags_of(flat_ref, bag_ref, k):
+    start = jnp.minimum((flat_ref[k * BLOCK] // 16) * 16, LAST_START)
+    start = pl.multiple_of(start, 16)
+    in_bag = [one_hot(WINDOW, WINDOW // 2, bag_ref[pl.ds(2 * k + j, 1), :] - start) for j in range(2)]
+    return start, jnp.concatenate(in_bag, axis=1)
+
+
+def count_slots(base, flat_ref, look_ref, bag_ref, acc_ref):
     acc_ref[...] = jnp.zeros_like(acc_ref)
-
-    def body(k, _):
-        start, in_bag = bags_of(first_ref, bag_ref, k)
-        slots = look_ref[pl.ds(k, 1), :] - HOT
-        in_slot = (lax.broadcasted_iota(i32, (UNIQ, BLOCK), 0) == slots).astype(f32).astype(bf16)
-        acc_ref[pl.ds(start, WINDOW), :] += mm_nt(in_bag, in_slot)
+    many = acc_ref.shape[1]
+
+    def body(q, _):
+        parts = []
+        for b in range(BATCH):
+            k = BATCH * q + b
+            start, in_bag = bags_of(flat_ref, bag_ref, k)
+            in_slot = [
+                one_hot(many, many // 2, look_ref[pl.ds(2 * k + j, 1), :] - (HOT + base))
+                for j in range(2)
+            ]
+            in_slot = jnp.concatenate(in_slot, axis=1)
+            parts.append((start, mm_nt(in_bag, in_slot).astype(bf16)))
+        for start, part in parts:
+            acc_ref[pl.ds(start, WINDOW), :] += part
         return 0
 
-    lax.fori_loop(0, BLOCKS, body, 0)
-    counts_ref[...] = acc_ref[0:BAGS, :].astype(bf16)
-
-
-def slot_counts(first, look, bags):
+    lax.fori_loop(0, BLOCKS // BATCH, body, 0)
+
+
+def counts_out(acc_ref, counts_ref, sems):
+    return [
+        pltpu.make_async_copy(
+            acc_ref.at[pl.ds(c * 512, 512)], counts_ref.at[pl.ds(c * 512, 512)], sems.at[c]
+        )
+        for c in range(4)
+    ]
+
+
+def counts_kernel(flat_ref, look_ref, bag_ref, counts_ref, acc_ref, sems):
+    count_slots(0, flat_ref, look_ref, bag_ref, acc_ref)
+    copies = counts_out(acc_ref, counts_ref, sems)
+    for copy in copies:
+        copy.start()
+    for copy in copies:
+        copy.wait()
+
+
+def slot_counts(flat, look, bags):
     return pl.pallas_call(
         counts_kernel,
-        out_shape=shape((BAGS, UNIQ), bf16),
+        out_shape=shape((BAGS, UNIQ // 2), bf16),
         in_specs=[SMEM, VMEM, VMEM],
-        out_specs=VMEM,
-        scratch_shapes=[pltpu.VMEM((PADDED, UNIQ), f32)],
-        compiler_params=params(18),
+        out_specs=HBM,
+        scratch_shapes=[pltpu.VMEM((BAGS, UNIQ // 2), bf16), pltpu.SemaphoreType.DMA((4,))],
+        compiler_params=params(58),
         cost_estimate=cost(5 * 10**9, 8 * MIB),
         name="counts",
-    )(first, look, bags)
-
-
-def bags_of(first_ref, bag_ref, k):
-    start = pl.multiple_of((first_ref[k] // 16) * 16, 16)
-    bags = bag_ref[pl.ds(k, 1), :] - start
-    in_bag = lax.broadcasted_iota(i32, (WINDOW, BLOCK), 0) == bags
-    return start, in_bag.astype(f32).astype(bf16)
+    )(flat, look, bags)
 
 
 CHUNKS = 8
 
 
 def pool_kernel(
-    first_ref, look_ref, bag_ref, slab_ref, pooled_ref, slab_vmem, table_ref, rows_ref, acc_ref, sems
+    flat_ref,
+    look_ref,
+    raw_ref,
+    bag_ref,
+    slab_ref,
+    pooled_ref,
+    counts_ref,
+    slab_vmem,
+    table_ref,
+    rows_ref,
+    counts_vmem,
+    sems,
+    count_sems,
 ):
     height = HOT // CHUNKS
 
@@ -175,7 +234,11 @@
 
     for c in range(CHUNKS):
         copy(c).start()
-    acc_ref[...] = jnp.zeros_like(acc_ref)
+    count_slots(UNIQ // 2, flat_ref, raw_ref, bag_ref, counts_vmem)
+    out_copies = counts_out(counts_vmem, counts_ref, count_sems)
+    for out_copy in out_copies:
+        out_copy.start()
+    pooled_ref[...] = jnp.zeros_like(pooled_ref)
     table_ref[HOT:, :] = jnp.zeros((GROUP, EMB), f32)
     for c in range(CHUNKS):
         copy(c).wait()
@@ -199,40 +262,43 @@
         parts = []
         for j in range(BATCH):
             k = q * BATCH + j
-            start, in_bag = bags_of(first_ref, bag_ref, k)
+            start, in_bag = bags_of(flat_ref, bag_ref, k)
             rows = rows_ref[pl.ds(pl.multiple_of(k * BLOCK, BLOCK), BLOCK), :].astype(bf16)
             parts.append((start, mm(in_bag, rows)))
         for start, part in parts:
-            acc_ref[pl.ds(start, WINDOW), :] += part
+            pooled_ref[pl.ds(start, WINDOW), :] += part
         return 0
 
     lax.fori_loop(0, BLOCKS // BATCH, batch, 0)
-    pooled_ref[...] = acc_ref[0:BAGS, :]
-
-
-def pool_hot(first, look, bags, slab):
+    for out_copy in out_copies:
+        out_copy.wait()
+
+
+def pool_hot(flat, look, raw, bags, slab):
     return pl.pallas_call(
         pool_kernel,
-        out_shape=shape((BAGS, EMB), f32),
-        in_specs=[SMEM, SMEM, VMEM, HBM],
-        out_specs=VMEM,
+        out_shape=(shape((BAGS, EMB), f32), shape((BAGS, UNIQ // 2), bf16)),
+        in_specs=[SMEM, SMEM, VMEM, VMEM, HBM],
+        out_specs=[VMEM, HBM],
         scratch_shapes=[
             pltpu.VMEM((HOT, EMB), bf16),
             pltpu.VMEM((HOT + GROUP, EMB), f32),
             pltpu.VMEM((LOOK, EMB), f32),
-            pltpu.VMEM((PADDED, EMB), f32),
+            pltpu.VMEM((BAGS, UNIQ // 2), bf16),
             pltpu.SemaphoreType.DMA((CHUNKS,)),
+            pltpu.SemaphoreType.DMA((4,)),
         ],
-        compiler_params=params(33),
+        compiler_params=params(58),
         cost_estimate=cost(10**9, 40 * MIB),
         name="pool",
-    )(first, look, bags, slab)
+    )(flat, look, raw, bags, slab)
 
 
 def layer_kernel(
     pos_ref,
     pooled_ref,
-    counts_ref,
+    count_a_ref,
+    count_b_ref,
     returned_ref,
     target_ref,
     weight_ref,
@@ -243,7 +309,23 @@
     out_grad_ref,
     wide_ref,
     slots_ref,
+    counts_vmem,
+    weight_vmem,
+    grads_vmem,
+    factors_vmem,
+    sems,
 ):
+    half = UNIQ // 2
+    counts_in = [
+        pltpu.make_async_copy(ref, counts_vmem.at[:, pl.ds(c * half, half)], sems.at[4 * c])
+        for c, ref in enumerate((count_a_ref, count_b_ref))
+    ]
+    weight_in = pltpu.make_async_copy(weight_ref, weight_vmem, sems.at[1])
+    grads_out = pltpu.make_async_copy(grads_vmem, bag_grad_ref, sems.at[2])
+    factors_out = pltpu.make_async_copy(factors_vmem, factors_ref, sems.at[3])
+    for copy in counts_in:
+        copy.start()
+    weight_in.start()
     wide_ref[...] = returned_ref[...].astype(f32)
 
     def fetch(k, _):
@@ -253,27 +335,36 @@
         return 0
 
     lax.fori_loop(0, UNIQ // 16, fetch, 0)
-    counts = counts_ref[...]
-    bag_grad_ref[...] = pooled_ref[...] + mm(counts, slots_ref[...].astype(bf16))
+    for copy in counts_in:
+        copy.wait()
+    counts = counts_vmem[...]
+    grads_vmem[...] = pooled_ref[...] + mm(counts, slots_ref[...].astype(bf16))
     pooled_in = jnp.concatenate(
-        [bag_grad_ref[pl.ds(f, B_DEV, stride=FEAT), :] for f in range(FEAT)], axis=1
+        [grads_vmem[pl.ds(f, B_DEV, stride=FEAT), :] for f in range(FEAT)], axis=1
     ).astype(bf16)
-    weight = weight_ref[...]
+    weight_in.wait()
+    weight = weight_vmem[...]
     out_weight = out_weight_ref[...]
     preact = mm(pooled_in, weight)
     gate = jax.nn.sigmoid(preact)
     act = (preact * gate).astype(bf16).astype(f32)
     logits = jnp.sum(act * out_weight, axis=1, keepdims=True)
-    logit_grad = jax.nn.sigmoid(logits) - target_ref[...]
+    diagonal = lax.broadcasted_iota(i32, (B_DEV, B_DEV), 0) == lax.broadcasted_iota(
+        i32, (B_DEV, B_DEV), 1
+    )
+    target = jnp.sum(jnp.where(diagonal, target_ref[...], 0.0), axis=1, keepdims=True)
+    logit_grad = jax.nn.sigmoid(logits) - target
     out_grad_ref[...] = jnp.sum(act * logit_grad, axis=0, keepdims=True)
     act_grad = (logit_grad * out_weight * gate * (1.0 + preact * (1.0 - gate))).astype(bf16)
-    factors_ref[0] = pooled_in
-    factors_ref[1] = act_grad
+    factors_vmem[0] = pooled_in
+    factors_vmem[1] = act_grad
+    factors_out.start()
     input_grad = mm_nt(act_grad, weight)
     for f in range(FEAT):
-        bag_grad_ref[pl.ds(f, B_DEV, stride=FEAT), :] = input_grad[:, f * EMB : (f + 1) * EMB]
-
-    grads = bag_grad_ref[...]
+        grads_vmem[pl.ds(f, B_DEV, stride=FEAT), :] = input_grad[:, f * EMB : (f + 1) * EMB]
+
+    grads_out.start()
+    grads = grads_vmem[...]
     high = grads.astype(bf16)
     low = (grads - high.astype(f32)).astype(bf16)
     both = mm_tn(counts, jnp.concatenate([high, low], axis=1))
@@ -288,9 +379,11 @@
 
     lax.fori_loop(0, UNIQ // 16, put, 0)
     outgoing_ref[...] = wide_ref[...].astype(bf16)
-
-
-def layer(pos, pooled, counts, returned, target, weight, out_weight):
+    grads_out.wait()
+    factors_out.wait()
+
+
+def layer(pos, pooled, count_a, count_b, returned, target, weight, out_weight):
     return pl.pallas_call(
         layer_kernel,
         out_shape=(
@@ -299,13 +392,21 @@
             shape((2, B_DEV, HID), bf16),
             shape((1, HID), f32),
         ),
-        in_specs=[SMEM] + [VMEM] * 6,
-        out_specs=[VMEM] * 4,
-        scratch_shapes=[pltpu.VMEM((SLOTS, EMB), f32), pltpu.VMEM((UNIQ, EMB), f32)],
-        compiler_params=params(30),
+        in_specs=[SMEM, VMEM, HBM, HBM, VMEM, VMEM, HBM, VMEM],
+        out_specs=[HBM, VMEM, HBM, VMEM],
+        scratch_shapes=[
+            pltpu.VMEM((SLOTS, EMB), f32),
+            pltpu.VMEM((UNIQ, EMB), f32),
+            pltpu.VMEM((BAGS, UNIQ), bf16),
+            pltpu.VMEM((HID, HID), bf16),
+            pltpu.VMEM((BAGS, EMB), f32),
+            pltpu.VMEM((2, B_DEV, HID), bf16),
+            pltpu.SemaphoreType.DMA((5,)),
+        ],
+        compiler_params=params(50),
         cost_estimate=cost(4 * 10**9, 20 * MIB),
         name="layer",
-    )(pos, pooled, counts, returned, target, weight, out_weight)
+    )(pos, pooled, count_a, count_b, returned, target, weight, out_weight)
 
 
 def hidden_kernel(mine_ref, one_ref, two_ref, hidden_ref):
@@ -332,18 +433,34 @@
 
 
 def scatter_kernel(
-    look_ref, clash_ref, clashes_ref, first_ref, mine_ref, bag_ref, grad_ref, keep_ref, send_ref, acc_ref, halves_ref, rows_ref
+    look_ref,
+    clash_ref,
+    flat_ref,
+    mine_ref,
+    bag_ref,
+    grad_ref,
+    keep_ref,
+    send_ref,
+    acc_ref,
+    halves_ref,
+    rows_ref,
+    grad_vmem,
+    keep_vmem,
+    send_vmem,
+    sems,
 ):
-    grads = grad_ref[...]
+    grads_in = pltpu.make_async_copy(grad_ref, grad_vmem, sems.at[0, 0])
+    grads_in.start()
+    grads_in.wait()
+    grads = grad_vmem[...]
     high, low = split(grads)
-    halves_ref[0:BAGS, 0:EMB] = high
-    halves_ref[0:BAGS, EMB:] = low
-    halves_ref[BAGS:, :] = jnp.zeros((PADDED - BAGS, 2 * EMB), bf16)
+    halves_ref[:, 0:EMB] = high
+    halves_ref[:, EMB:] = low
 
     def stage(q, _):
         for j in range(BATCH):
             k = q * BATCH + j
-            start, in_bag = bags_of(first_ref, bag_ref, k)
+            start, in_bag = bags_of(flat_ref, bag_ref, k)
             both = mm_tn(in_bag, halves_ref[pl.ds(start, WINDOW), :])
             rows_ref[pl.ds(pl.multiple_of(k * BLOCK, BLOCK), BLOCK), :] = (
                 both[:, :EMB] + both[:, EMB:]
@@ -366,20 +483,22 @@
             acc_ref[pl.ds(rows[m], 1), :] = sums[m]
 
     def block(k, _):
-        @pl.when(clashes_ref[k] == 0)
+        clashes = clash_ref[k * FLAGS + ANY]
+
+        @pl.when(clashes == 0)
         def _():
             def pair(q, _):
-                distinct(k * BLOCK + q * 2 * GROUP)
-                distinct(k * BLOCK + q * 2 * GROUP + GROUP)
+                distinct(k * 128 + q * 2 * GROUP)
+                distinct(k * 128 + q * 2 * GROUP + GROUP)
                 return 0
 
-            lax.fori_loop(0, BLOCK // GROUP // 2, pair, 0)
-
-        @pl.when(clashes_ref[k] != 0)
+            lax.fori_loop(0, 128 // GROUP // 2, pair, 0)
+
+        @pl.when(clashes != 0)
         def _():
             def group(q, _):
-                at = k * BLOCK + q * GROUP
-                clash = clash_ref[k * (BLOCK // GROUP) + q]
+                at = k * 128 + q * GROUP
+                clash = clash_ref[k * FLAGS + q]
 
                 @pl.when(clash == 0)
                 def _():
@@ -392,14 +511,24 @@
 
                 return 0
 
-            lax.fori_loop(0, BLOCK // GROUP, group, 0)
+            lax.fori_loop(0, 128 // GROUP, group, 0)
 
         return 0
 
-    lax.fori_loop(0, BLOCKS, block, 0)
+    lax.fori_loop(0, LOOK // 128, block, 0)
 
     core, bits = mine_ref[1], mine_ref[2]
+
+    def copies(s):
+        return (
+            pltpu.make_async_copy(send_vmem.at[s % 2], send_ref.at[s], sems.at[s % 2, 0]),
+            pltpu.make_async_copy(keep_vmem.at[s % 2], keep_ref.at[s], sems.at[s % 2, 1]),
+        )
+
     for s in range(4):
+        if s >= 2:
+            for copy in copies(s - 2):
+                copy.wait()
 
         def gather(k, _, s=s):
             bit = [(bits >> (3 - axis)) & 1 for axis in range(4)]
@@ -411,28 +540,37 @@
             own = pl.multiple_of(base + 512 * core, 32)
             other = pl.multiple_of(base + 512 * (1 - core), 32)
             for z in range(8):
-                keep_ref[s, k, z] = acc_ref[pl.ds(own + z * 4096, 32), :]
-                send_ref[s, k, z] = acc_ref[pl.ds(other + z * 4096, 32), :].astype(bf16)
+                keep_vmem[s % 2, k, z] = acc_ref[pl.ds(own + z * 4096, 32), :]
+                send_vmem[s % 2, k, z] = acc_ref[pl.ds(other + z * 4096, 32), :].astype(bf16)
             return 0
 
         lax.fori_loop(0, 16, gather, 0)
-
-
-def scatter_hot(look, clash, clashes, first, mine, bags, grads):
+        for copy in copies(s):
+            copy.start()
+    for s in (2, 3):
+        for copy in copies(s):
+            copy.wait()
+
+
+def scatter_hot(look, clash, flat, mine, bags, grads):
     return pl.pallas_call(
         scatter_kernel,
         out_shape=(shape((4, 16, 8, 32, EMB), f32), shape((4, 16, 8, 32, EMB), bf16)),
-        in_specs=[SMEM] * 5 + [VMEM] * 2,
-        out_specs=[VMEM] * 2,
+        in_specs=[SMEM] * 4 + [VMEM, HBM],
+        out_specs=[HBM] * 2,
         scratch_shapes=[
             pltpu.VMEM((HOT + GROUP, EMB), f32),
-            pltpu.VMEM((PADDED, 2 * EMB), bf16),
+            pltpu.VMEM((BAGS, 2 * EMB), bf16),
             pltpu.VMEM((LOOK, EMB), f32),
+            pltpu.VMEM((BAGS, EMB), f32),
+            pltpu.VMEM((2, 16, 8, 32, EMB), f32),
+            pltpu.VMEM((2, 16, 8, 32, EMB), bf16),
+            pltpu.SemaphoreType.DMA((2, 2)),
         ],
-        compiler_params=params(40),
+        compiler_params=params(58),
         cost_estimate=cost(10**9, 80 * MIB),
         name="scatter",
-    )(look, clash, clashes, first, mine, bags, grads)
+    )(look, clash, flat, mine, bags, grads)
 
 
 def split(values):
@@ -665,7 +803,21 @@
 
 
 def update_kernel(
-    recv_ref, slab_ref, accum_ref, weight_ref, hid_accum_ref, new_ref, accum_new_ref, weight_new_ref, hid_new_ref, out_ref
+    place_ref,
+    recv_ref,
+    slab_ref,
+    accum_ref,
+    weight_ref,
+    hid_accum_ref,
+    out_weight_ref,
+    out_accum_ref,
+    new_ref,
+    accum_new_ref,
+    weight_new_ref,
+    hid_new_ref,
+    out_new_ref,
+    out_accum_new_ref,
+    out_ref,
 ):
     total = jnp.sum(recv_ref[...].astype(f32), axis=0)
     new_ref[...], accum_new_ref[...] = row_update(
@@ -679,9 +831,14 @@
         hid_new_ref[:, columns] = accum_new
         weight_new_ref[:, columns] = weight_ref[:, columns] - learn_rate * grad / jnp.sqrt(accum_new)
     out_ref[...] = total[320:328] + total[328:336]
-
-
-def update_owned(recv, slab, accum, weight, hid_accum):
+    row = out_ref[pl.ds(place_ref[1], 1), :]
+    grad = pltpu.roll(row, place_ref[2], 1)[:, 0:4]
+    accum_new = out_accum_ref[...] + grad * grad
+    out_accum_new_ref[...] = accum_new
+    out_new_ref[...] = out_weight_ref[...] - learn_rate * grad / jnp.sqrt(accum_new)
+
+
+def update_owned(place, recv, slab, accum, weight, hid_accum, out_weight, out_accum):
     return pl.pallas_call(
         update_kernel,
         out_shape=(
@@ -689,13 +846,15 @@
             shape((1, 128), f32),
             shape((4, HID), f32),
             shape((4, HID), f32),
-            shape((8, EMB), f32),
+            shape((1, 4), f32),
+            shape((1, 4), f32),
         ),
-        in_specs=[VMEM] * 5,
-        out_specs=[VMEM] * 5,
+        in_specs=[SMEM] + [VMEM] * 7,
+        out_specs=[VMEM] * 6,
+        scratch_shapes=[pltpu.VMEM((8, EMB), f32)],
         compiler_params=params(16),
         name="update",
-    )(recv, slab, accum, weight, hid_accum)
+    )(place, recv, slab, accum, weight, hid_accum, out_weight, out_accum)
 
 
 def cold_grad_kernel(asked_ref, incoming_ref, a_ref, b_ref):
@@ -787,10 +946,12 @@
     return lax.ppermute(value, "dp", pairs)
 
 
+Z_GROUPS = [[dp_index(z, x, core) for z in range(8)] for x in range(4) for core in range(2)]
+
+
 def over_z(value):
-    groups = [[dp_index(z, x, core) for z in range(8)] for x in range(4) for core in range(2)]
     return lax.all_to_all(
-        value, "dp", split_axis=0, concat_axis=0, tiled=True, axis_index_groups=groups
+        value, "dp", split_axis=0, concat_axis=0, tiled=True, axis_index_groups=Z_GROUPS
     )
 
 
@@ -814,34 +975,38 @@
     core, x = dp & 1, (dp >> 1) & 3
     position = dp * 4 + y
     bits = ((x ^ (x >> 1)) << 2) | (y ^ (y >> 1))
+    place = jnp.stack([position * 128, position >> 5, (128 - (position & 31) * 4) & 127]).astype(i32)
     mine = jnp.stack([(core << 9) | (bits << 5), core, bits]).astype(i32)
 
     rows = LOOK // 128
-    look = lookup_index.reshape(rows, 128)
-    spare = HOT + (lax.broadcasted_iota(i32, (rows, 128), 1) & (GROUP - 1))
-    look = jnp.where(look < HOT, look, spare)
-    look_flat = look.reshape(LOOK)
-    bag_rows = bag_id.reshape(BLOCKS, BLOCK)
-    first = bag_rows[:, 0]
-
-    requests, pos, clash = route(
-        touched_owner.reshape(1, UNIQ), touched_row.reshape(1, UNIQ), look
-    )
+    look_rows = lookup_index.reshape(rows, 128)
+    bag_flat = bag_id.reshape(LOOK)
+    bag_rows = bag_id.reshape(rows, 128)
+
+    requests, pos = route(touched_owner.reshape(1, UNIQ), touched_row.reshape(1, UNIQ))
     pos_flat = pos.reshape(UNIQ)
-    counts = slot_counts(first, lookup_index.reshape(BLOCKS, BLOCK), bag_rows)
+    look_hot, clash = clashes(look_rows)
+    look_flat, clash = look_hot.reshape(LOOK), clash.reshape(rows * FLAGS)
+    count_a = slot_counts(bag_flat, look_rows, bag_rows)
     asked = lax.all_to_all(requests, "dp", split_axis=0, concat_axis=0, tiled=True)
-    asked, counts = lax.optimization_barrier((asked, counts))
-    found = found_rows(jnp.maximum(asked, 0).reshape(SLOTS), cold_table)
+    asked, count_a, mine, place, clash, pos_flat, look_flat = lax.optimization_barrier(
+        (asked, count_a, mine, place, clash, pos_flat, look_flat)
+    )
+    found = found_rows(asked, cold_table)
     returned = lax.all_to_all(
         found.reshape(N_DP, CAP, EMB), "dp", split_axis=0, concat_axis=0, tiled=True
     ).reshape(SLOTS, EMB)
-    pooled = pool_hot(first, look_flat, bag_rows, hot_slab)
+    pooled, count_b = pool_hot(bag_flat, look_flat, look_rows, bag_rows, hot_slab)
+    pooled, count_b, asked_row = lax.optimization_barrier(
+        (pooled, count_b, asked.reshape(1, SLOTS))
+    )
     bag_grad, outgoing, factors, out_grad = layer(
         pos_flat,
         pooled,
-        counts,
+        count_a,
+        count_b,
         returned,
-        labels.reshape(B_DEV, 1),
+        labels.reshape(1, B_DEV),
         w_hidden,
         w_out.reshape(1, HID),
     )
@@ -851,15 +1016,14 @@
     other_factors = over_core(factors)
     out_grad = out_grad.reshape(8, EMB)
     out_recv = over_core(out_grad)
-    clashes = jnp.max(clash.reshape(BLOCKS, BLOCK // GROUP), axis=1)
-    keep, send = scatter_hot(
-        look_flat, clash.reshape(LOOK // GROUP), clashes, first, mine, bag_rows, bag_grad
-    )
-    send, incoming = lax.optimization_barrier((send, incoming))
+    keep, send = scatter_hot(look_flat, clash, bag_flat, mine, bag_rows, bag_grad)
+    send, incoming, other_factors, out_recv = lax.optimization_barrier(
+        (send, incoming, other_factors, out_recv)
+    )
     recv = over_core(send)
+    cold_a, cold_b = cold_grads(asked_row, incoming)
+    recv_a, recv_b = over_axis(cold_a, 3), over_axis(cold_b, 2)
     hidden = hidden_half(mine, factors, other_factors)
-    cold_a, cold_b = cold_grads(asked.reshape(1, SLOTS), incoming)
-    recv_a, recv_b = over_axis(cold_a, 3), over_axis(cold_b, 2)
     sends = first_send(keep, recv, hidden, out_grad, out_recv)
     recv_a, recv_b, *sends = lax.optimization_barrier((recv_a, recv_b, *sends))
     keeps = first_keep(keep, recv, hidden)
@@ -867,8 +1031,9 @@
         travelled = [over_axis(sends[s], ORDERS[s][step]) for s in range(4)] + [sends[4]]
         if step < 3:
             sends, keeps = next_step(step + 1, travelled, keeps)
+    parts = last_step(travelled, keeps)
     pair_a, pair_b = pair_sums(cold_a, recv_a, cold_b, recv_b)
-    parts, pair_a, pair_b = lax.optimization_barrier((last_step(travelled, keeps), pair_a, pair_b))
+    parts, pair_a, pair_b = lax.optimization_barrier((parts, pair_a, pair_b))
     recv_a, recv_b = over_axis(pair_a, 2), over_axis(pair_b, 3)
     parts = over_z(parts)
     cold_new, cold_accum_new = update_cold(
@@ -878,12 +1043,16 @@
     own_slab = lax.dynamic_slice_in_dim(hot_slab, position * 128, 128, 0)
     own_hidden = lax.dynamic_slice_in_dim(w_hidden, position * 4, 4, 0).astype(f32)
     own_out = lax.dynamic_slice_in_dim(w_out, position * 4, 4, 0)
-    hot_new, hot_accum_new, hidden_new, hidden_accum_new, out_total = update_owned(
-        parts, own_slab, hot_accum.reshape(1, 128), own_hidden, hidden_accum
-    )
-    out_part = lax.dynamic_slice_in_dim(out_total.reshape(HID), position * 4, 4, 0)
-    out_accum_new = out_accum + out_part * out_part
-    out_new = own_out - learn_rate * out_part / jnp.sqrt(out_accum_new)
+    hot_new, hot_accum_new, hidden_new, hidden_accum_new, out_new, out_accum_new = update_owned(
+        place,
+        parts,
+        own_slab,
+        hot_accum.reshape(1, 128),
+        own_hidden,
+        hidden_accum,
+        own_out.reshape(1, 4),
+        out_accum.reshape(1, 4),
+    )
     return (
         hot_new,
         hot_accum_new.reshape(128),
@@ -891,8 +1060,8 @@
         cold_accum_new.reshape(R_OWN),
         hidden_new,
         hidden_accum_new,
-        out_new,
-        out_accum_new,
+        out_new.reshape(4),
+        out_accum_new.reshape(4),
     )
 
 

time: 224 us -> 211 us (0.942)
  local copies, waits for them, and re-layouts: 21.8 us -> 7.1 us
  Pallas kernels: 80.2 us -> 85.6 us
  starting transfers between devices: 65.9 us -> 62.6 us
  other arithmetic: 3.88 us -> 1.28 us
    unnamed x45 -> x40, local copies, waits for them, and re-layouts: 19.6 us -> 6.17 us
    pallas_call x1, Pallas kernels: 20.3 us -> 28.8 us  [scatter_hot(): pl.pallas_call(scatter_kernel, out_shape=(shape((4, 16, 8, 32, EMB), f32)...]
    ppermute x12, starting transfers between devices: 17.3 us -> 14.2 us  [over_axis(): return lax.ppermute(value, 'rep', [(y, swap(y)) for y in range(4)])]
    ppermute x12, waiting for transfers between devices: 30.7 us -> 33.1 us  [over_axis(): return lax.ppermute(value, 'rep', [(y, swap(y)) for y in range(4)])]
    pallas_call x1, Pallas kernels: 2.81 us -> 0.51 us  [first_keep(): pl.pallas_call(first_keep_kernel, out_shape=keep_shapes(8), in_specs=[VME...]
    pallas_call x1, Pallas kernels: 2.89 us -> 0.61 us  [first_send(): pl.pallas_call(first_send_kernel, out_shape=send_shapes(8), in_specs=[VME...]
    pallas_call x2 -> x3, Pallas kernels: 26.4 us -> 26.1 us  [the longest x1 18.8 us: pool_hot(): pl.pallas_call(pool_kernel, out_shape=(shape((BAGS, EMB), f32), shape((BA...]
  transfers between devices with their start and end apart: 27 -> 27, of which waited for: 16 -> 19; matrix products, arithmetic and copies ran while one was open for 2% -> 1% of each run, Pallas kernels for 27% -> 30%
where the time goes in v2:
time: 211 us; the launch traced here: 209 us
  Pallas kernels  85.6 us (41%)
  starting transfers between devices  62.6 us (30%)
  waiting for transfers between devices  51.3 us (24%)
  local copies, waits for them, and re-layouts  7.1 us (3%)
    ppermute x12, waiting for transfers between devices, over_axis(): return lax.ppermute(value, 'rep', [(y, swap(y)) for y in range(4)])  33.1 us
    pallas_call x1, Pallas kernels, scatter_hot(): pl.pallas_call(scatter_kernel, out_shape=(shape((4, 16, 8, 32, EMB), f32)...  28.8 us
    pallas_call x1, Pallas kernels, pool_hot(): pl.pallas_call(pool_kernel, out_shape=(shape((BAGS, EMB), f32), shape((BA...  18.8 us
    ppermute x12, starting transfers between devices, over_axis(): return lax.ppermute(value, 'rep', [(y, swap(y)) for y in range(4)])  14.2 us
    ppermute x8, starting transfers between devices, over_axis(): return lax.ppermute(value, 'dp', pairs)  12.4 us
    pallas_call x1, Pallas kernels, layer(): pl.pallas_call(layer_kernel, out_shape=(shape((BAGS, EMB), f32), shape((S...  12.4 us
    all_to_all x1, starting transfers between devices, on_device(): lax.all_to_all(requests, 'dp', split_axis=0, concat_axis=0, tiled=True)  12 us
    all_to_all x1, starting transfers between devices, on_device(): lax.all_to_all(found.reshape(N_DP, CAP, EMB), 'dp', split_axis=0, concat_...  10.2 us
  transfers between devices with their start and end apart: 27, of which 19 were waited for; matrix products, arithmetic and copies ran while one was open for 1% of the time, Pallas kernels for 30%

profile of v2, /device:TPU:2, one launch (start us, length us, event | category | flops | bytes accessed | tf_op | source)
XLA Modules:
  0.0 208.8 jit_solution(9577426035224939167)
XLA Ops:
  3.2 12.0 %all-to-all-start = ((s32[64,1,48]{2,1,0:T(1,128)}), s32[64,1,48]{2,1,0:T(1,128)S(1)}, u32[]{:S(2)}, u32[]{:S(2)}) async-start(s32[64,1,48]{2,1,0:T(1,128)} %bitcast.3), calls=%async_computation | async-start | bytes 65536 | tf_op jit(solution)/shard_map/all_to_all | solution.py:991
  15.3 6.9 %counts.1.count_a_ref = bf16[2048,512]{1,0:T(8,128)(2,1)} custom-call(s32[8192]{0:T(1024)} %bitcast.56, s32[64,128]{1,0:T(8,128)} %bitcast.40, s32[64,128]{1,0:T(8,128)} %bitcast.57), custom_call_target="tpu_custom_call" | custom-call | flops 5000000000 | bytes 8388608 | tf_op jit(solution)/shard_map/counts/pallas_call | solution.py:199
  23.8 4.8 %found.1 = bf16[3072,128]{1,0:T(8,128)(2,1)} custom-call(s32[64,48]{1,0:T(8,128)S(1)} %bitcast.38, f32[2048,128]{1,0:T(8,128)S(1)} %copy-done), custom_call_target="tpu_custom_call" | custom-call | tf_op jit(solution)/shard_map/found/pallas_call | solution.py:133
  28.6 10.2 %all-to-all-start.1 = ((bf16[64,48,128]{2,1,0:T(8,128)(2,1)}), bf16[64,48,128]{2,1,0:T(8,128)(2,1)S(1)}, u32[]{:S(2)}, u32[]{:S(2)}) async-start(bf16[64,48,128]{2,1,0:T(8,128)(2,1)} %bitcast.17), calls=%async_computation.1 | async-start | bytes 1572864 | tf_op jit(solution)/shard_map/all_to_all | solution.py:996
  39.0 18.8 %pool.1 = (f32[2048,128]{1,0:T(8,128)}, bf16[2048,512]{1,0:T(8,128)(2,1)}) custom-call(s32[8192]{0:T(1024)} %bitcast.58, s32[8192]{0:T(1024)} %bitcast.43, s32[64,128]{1,0:T(8,128)} %bitcast.41, s32[64,128]{1,0:T(8,128)} %bitcast.59, bf16[32768,128]{1,0:T(8,128)(2,1)} %slab_ref.1), custom_call_target="tpu_custom_call" | custom-call | flops 1000000000 | bytes 41943040 | tf_op jit(solution)/shard_map/pool/pallas_call | solution.py:278
  57.8 4.2 %all-to-all-done.1 = bf16[64,48,128]{2,1,0:T(8,128)(2,1)S(1)} async-done(((bf16[64,48,128]{2,1,0:T(8,128)(2,1)}), bf16[64,48,128]{2,1,0:T(8,128)(2,1)S(1)}, u32[]{:S(2)}, u32[]{:S(2)}) %all-to-all-start.1) | async-done | bytes 786464 | tf_op jit(solution)/shard_map/all_to_all | solution.py:996
  62.0 12.4 %layer.1 = (f32[2048,128]{1,0:T(8,128)S(1)}, bf16[3072,128]{1,0:T(8,128)(2,1)}, bf16[2,256,1024]{2,1,0:T(8,128)(2,1)S(1)}, f32[1,1024]{1,0:T(1,128)S(1)}) custom-call(s32[1024]{0:T(1024)S(1)} %bitcast.54, f32[2048,128]{1,0:T(8,128)} %get-tuple-element.121.pooled_ref, bf16[2048,512]{1,0:T(8,128)(2,1)} %counts.1.count_a_ref, ...), custom_call_target="tpu_custom_call" | custom-call | flops 4000000000 | bytes 20971520 | tf_op jit(solution)/shard_map/layer/pallas_call | solution.py:387
  76.4 6.1 %all-to-all-start.2 = ((bf16[64,48,128]{2,1,0:T(8,128)(2,1)}), bf16[64,48,128]{2,1,0:T(8,128)(2,1)S(1)}, u32[]{:S(2)}, u32[]{:S(2)}) async-start(bf16[64,48,128]{2,1,0:T(8,128)(2,1)} %bitcast.21), calls=%async_computation.2 | async-start | bytes 1572864 | tf_op jit(solution)/shard_map/all_to_all | solution.py:1013
  83.3 28.8 %scatter.1 = (f32[4,16,8,32,128]{4,3,2,1,0:T(8,128)}, bf16[4,16,8,32,128]{4,3,2,1,0:T(8,128)(2,1)}) custom-call(s32[8192]{0:T(1024)} %bitcast.44, s32[8192]{0:T(1024)} %bitcast.52, s32[8192]{0:T(1024)} %bitcast.60, s32[3]{0:T(128)} %get-tuple-element.119.mine_ref, s32[64,128]{1,0:T(8,128)} %bitcast.61, f32[2048,128]{1,0:T(8,128)} %copy-done.17), custom_call_target="tpu_custom_call" | custom-call | flops 1000000000 | bytes 83886080 | tf_op jit(solution)/shard_map/scatter/pallas_call | solution.py:556
  113.2 3.4 %cold_grads.1 = (bf16[1024,128]{1,0:T(8,128)(2,1)S(1)}, bf16[1024,128]{1,0:T(8,128)(2,1)S(1)}) custom-call(s32[1,3072]{1,0:T(1,128)S(1)} %reshape.98.asked_ref, bf16[3072,128]{1,0:T(8,128)(2,1)S(1)} %bitcast.36), custom_call_target="tpu_custom_call" | custom-call | flops 2000000000 | bytes 4194304 | tf_op jit(solution)/shard_map/cold_grads/pallas_call | solution.py:873
  117.1 2.5 %collective-permute-start.3 = (bf16[1024,128]{1,0:T(8,128)(2,1)S(1)}, bf16[1024,128]{1,0:T(8,128)(2,1)S(1)}, u32[]{:S(2)}, u32[]{:S(2)}) collective-permute-start(bf16[1024,128]{1,0:T(8,128)(2,1)S(1)} %get-tuple-element.131.c), channel_id=1, source_target_pairs={{0,3},{1,2},{2,1},{3,0},{4,7},{5,6},{6,5},{7,4},{8,11},{9,10},{10,... | collective-permute-start | bytes 786440 | tf_op jit(solution)/shard_map/ppermute | solution.py:939
  120.8 2.1 %hidden_half.1.hidden_ref = f32[512,1024]{1,0:T(8,128)S(1)} custom-call(s32[3]{0:T(128)S(1)} %copy-done.7, bf16[2,256,1024]{2,1,0:T(8,128)(2,1)S(1)} %copy-done.11, bf16[2,256,1024]{2,1,0:T(8,128)(2,1)S(1)} %copy-done.13), custom_call_target="tpu_custom_call" | custom-call | flops 4000000000 | bytes 4194304 | tf_op jit(solution)/shard_map/hidden_half/pallas_call | solution.py:424
  123.6 1.8 collective-permute-done.2.b
  127.2 2.0 collective-permute-start.6
  129.2 1.7 collective-permute-start.7
  132.7 14.2 %collective-permute-done.6.refs_1_ = bf16[3072,128]{1,0:T(8,128)(2,1)S(1)} collective-permute-done((bf16[3072,128]{1,0:T(8,128)(2,1)S(1)}, bf16[3072,128]{1,0:T(8,128)(2,1)S(1)}, u32[]{:S(2)}, u32[]{:S(2)}) %collective-permute-start.6) | collective-permute-done | bytes 786464 | tf_op jit(solution)/shard_map/ppermute | solution.py:939
  151.2 1.7 collective-permute-start.11
  152.9 2.1 %collective-permute-start.12 = (bf16[1536,128]{1,0:T(8,128)(2,1)S(1)}, bf16[1536,128]{1,0:T(8,128)(2,1)S(1)}, u32[]{:S(2)}, u32[]{:S(2)}) collective-permute-start(bf16[1536,128]{1,0:T(8,128)(2,1)S(1)} %get-tuple-element.157), channel_id=1, source_target_pairs={{0,8},{4,12},{8,0},{12,4},{16,24},{20,28},{24,16},{28,20},{32,40},... | collective-permute-start | bytes 1179656 | tf_op jit(solution)/shard_map/ppermute | solution.py:946
  155.0 4.5 %collective-permute-done.10.refs_1_ = bf16[1536,128]{1,0:T(8,128)(2,1)S(1)} collective-permute-done((bf16[1536,128]{1,0:T(8,128)(2,1)S(1)}, bf16[1536,128]{1,0:T(8,128)(2,1)S(1)}, u32[]{:S(2)}, u32[]{:S(2)}) %collective-permute-start.10) | collective-permute-done | bytes 393248 | tf_op jit(solution)/shard_map/ppermute | solution.py:939
  159.9 1.9 collective-permute-done.12.refs_3_
  162.1 2.1 %collective-permute-start.13 = (bf16[1296,128]{1,0:T(8,128)(2,1)S(1)}, bf16[1296,128]{1,0:T(8,128)(2,1)S(1)}, u32[]{:S(2)}, u32[]{:S(2)}) collective-permute-start(bf16[1296,128]{1,0:T(8,128)(2,1)S(1)} %get-tuple-element.167), channel_id=1, source_target_pairs={{0,8},{4,12},{8,0},{12,4},{16,24},{20,28},{24,16},{28,20},{32,40},... | collective-permute-start | bytes 995336 | tf_op jit(solution)/shard_map/ppermute | solution.py:946
  166.0 2.0 collective-permute-start.16
  168.0 3.3 %collective-permute-done.14.refs_1_ = bf16[1280,128]{1,0:T(8,128)(2,1)S(1)} collective-permute-done((bf16[1280,128]{1,0:T(8,128)(2,1)S(1)}, bf16[1280,128]{1,0:T(8,128)(2,1)S(1)}, u32[]{:S(2)}, u32[]{:S(2)}) %collective-permute-start.14) | collective-permute-done | bytes 327712 | tf_op jit(solution)/shard_map/ppermute | solution.py:946
  171.5 2.8 %collective-permute-done.16.refs_3_ = bf16[1280,128]{1,0:T(8,128)(2,1)S(1)} collective-permute-done((bf16[1280,128]{1,0:T(8,128)(2,1)S(1)}, bf16[1280,128]{1,0:T(8,128)(2,1)S(1)}, u32[]{:S(2)}, u32[]{:S(2)}) %collective-permute-start.16) | collective-permute-done | bytes 327712 | tf_op jit(solution)/shard_map/ppermute | solution.py:939
  174.6 1.9 collective-permute-start.17
  177.8 2.1 %collective-permute-start.19 = (bf16[640,128]{1,0:T(8,128)(2,1)S(1)}, bf16[640,128]{1,0:T(8,128)(2,1)S(1)}, u32[]{:S(2)}, u32[]{:S(2)}) collective-permute-start(bf16[640,128]{1,0:T(8,128)(2,1)S(1)} %get-tuple-element.182), channel_id=1, source_target_pairs={{0,3},{1,2},{2,1},{3,0},{4,7},{5,6},{6,5},{7,4},{8,11},{9,10},{10,... | collective-permute-start | bytes 491528 | tf_op jit(solution)/shard_map/ppermute | solution.py:939
  180.1 1.6 collective-permute-done.18.refs_1_
  181.7 2.6 %collective-permute-done.19.refs_2_ = bf16[640,128]{1,0:T(8,128)(2,1)S(1)} collective-permute-done((bf16[640,128]{1,0:T(8,128)(2,1)S(1)}, bf16[640,128]{1,0:T(8,128)(2,1)S(1)}, u32[]{:S(2)}, u32[]{:S(2)}) %collective-permute-start.19) | collective-permute-done | bytes 163872 | tf_op jit(solution)/shard_map/ppermute | solution.py:939
  186.3 6.9 %all-to-all-start.3 = ((bf16[8,336,128]{2,1,0:T(8,128)(2,1)}), bf16[8,336,128]{2,1,0:T(8,128)(2,1)S(1)}, u32[]{:S(2)}, u32[]{:S(2)}) async-start(bf16[8,336,128]{2,1,0:T(8,128)(2,1)} %step_5.1), calls=%async_computation.3 | async-start | bytes 1376256 | tf_op jit(solution)/shard_map/all_to_all | solution.py:953
  196.4 4.5 %collective-permute-done.21.b = bf16[1024,128]{1,0:T(8,128)(2,1)S(1)} collective-permute-done((bf16[1024,128]{1,0:T(8,128)(2,1)S(1)}, bf16[1024,128]{1,0:T(8,128)(2,1)S(1)}, u32[]{:S(2)}, u32[]{:S(2)}) %collective-permute-start.21) | collective-permute-done | bytes 262176 | tf_op jit(solution)/shard_map/ppermute | solution.py:939
  201.2 1.8 cold_update.1
  202.9 4.4 %all-to-all-done.3.recv_ref = bf16[8,336,128]{2,1,0:T(8,128)(2,1)S(1)} async-done(((bf16[8,336,128]{2,1,0:T(8,128)(2,1)}), bf16[8,336,128]{2,1,0:T(8,128)(2,1)S(1)}, u32[]{:S(2)}, u32[]{:S(2)}) %all-to-all-start.3) | async-done | bytes 688160 | tf_op jit(solution)/shard_map/all_to_all | solution.py:953
  (86 shorter events, 29.6 us)
Async XLA Ops:
  3.2 20.5 %all-to-all-start = ((s32[64,1,48]{2,1,0:T(1,128)}), s32[64,1,48]{2,1,0:T(1,128)S(1)}, u32[]{:S(2)}, u32[]{:S(2)}) async-start(s32[64,1,48]{2,1,0:T(1,128)} %bitcast.3), calls=%async_computation | async-start | bytes 65536 | tf_op jit(solution)/shard_map/all_to_all | solution.py:991
  23.7 34.1 %copy-start.14 = (s32[64,128]{1,0:T(8,128)}, s32[64,128]{1,0:T(8,128)S(1)}, u32[]{:S(2)}) copy-start(s32[64,128]{1,0:T(8,128)S(1)} %get-tuple-element.109) | copy-start | bytes 98308
  28.6 33.4 %all-to-all-start.1 = ((bf16[64,48,128]{2,1,0:T(8,128)(2,1)}), bf16[64,48,128]{2,1,0:T(8,128)(2,1)S(1)}, u32[]{:S(2)}, u32[]{:S(2)}) async-start(bf16[64,48,128]{2,1,0:T(8,128)(2,1)} %bitcast.17), calls=%async_computation.1 | async-start | bytes 1572864 | tf_op jit(solution)/shard_map/all_to_all | solution.py:996
  76.4 36.7 %all-to-all-start.2 = ((bf16[64,48,128]{2,1,0:T(8,128)(2,1)}), bf16[64,48,128]{2,1,0:T(8,128)(2,1)S(1)}, u32[]{:S(2)}, u32[]{:S(2)}) async-start(bf16[64,48,128]{2,1,0:T(8,128)(2,1)} %bitcast.21), calls=%async_computation.2 | async-start | bytes 1572864 | tf_op jit(solution)/shard_map/all_to_all | solution.py:1013
  82.5 29.6 %collective-permute-start = (bf16[2,256,1024]{2,1,0:T(8,128)(2,1)}, bf16[2,256,1024]{2,1,0:T(8,128)(2,1)S(1)}, u32[]{:S(2)}, u32[]{:S(2)}) collective-permute-start(bf16[2,256,1024]{2,1,0:T(8,128)(2,1)} %copy-done.10), channel_id=1, source_target_pairs={{0,4},{4,0},{8,12},{12,8},{16,20},{20,16},{24,28},{28,24},{32,36},... | collective-permute-start | bytes 3145736 | tf_op jit(solution)/shard_map/ppermute | solution.py:933
  83.0 29.2 %collective-permute-start.1 = (f32[8,128]{1,0:T(8,128)S(1)}, f32[8,128]{1,0:T(8,128)S(1)}, u32[]{:S(2)}, u32[]{:S(2)}) collective-permute-start(f32[8,128]{1,0:T(8,128)S(1)} %bitcast.46), channel_id=1, source_target_pairs={{0,4},{4,0},{8,12},{12,8},{16,20},{20,16},{24,28},{28,24},{32,36},... | collective-permute-start | bytes 12296 | tf_op jit(solution)/shard_map/ppermute | solution.py:933
  113.2 9.8 %collective-permute-start.4 = (bf16[4,16,8,32,128]{4,3,2,1,0:T(8,128)(2,1)}, bf16[4,16,8,32,128]{4,3,2,1,0:T(8,128)(2,1)S(1)}, u32[]{:S(2)}, u32[]{:S(2)}) collective-permute-start(bf16[4,16,8,32,128]{4,3,2,1,0:T(8,128)(2,1)} %get-tuple-element.133), channel_id=1, source_target_pairs={{0,4},{4,0},{8,12},{12,8},{16,20},{20,16},{24,28},{28,24},{32,36},... | collective-permute-start | bytes 12582920 | tf_op jit(solution)/shard_map/ppermute | solution.py:933
  116.6 8.8 %collective-permute-start.2 = (bf16[1024,128]{1,0:T(8,128)(2,1)S(1)}, bf16[1024,128]{1,0:T(8,128)(2,1)S(1)}, u32[]{:S(2)}, u32[]{:S(2)}) collective-permute-start(bf16[1024,128]{1,0:T(8,128)(2,1)S(1)} %get-tuple-element.130.a), channel_id=1, source_target_pairs={{0,1},{1,0},{2,3},{3,2},{4,5},{5,4},{6,7},{7,6},{8,9},{9,8},{10,11... | collective-permute-start | bytes 786440 | tf_op jit(solution)/shard_map/ppermute | solution.py:939
  117.1 9.6 %collective-permute-start.3 = (bf16[1024,128]{1,0:T(8,128)(2,1)S(1)}, bf16[1024,128]{1,0:T(8,128)(2,1)S(1)}, u32[]{:S(2)}, u32[]{:S(2)}) collective-permute-start(bf16[1024,128]{1,0:T(8,128)(2,1)S(1)} %get-tuple-element.131.c), channel_id=1, source_target_pairs={{0,3},{1,2},{2,1},{3,0},{4,7},{5,6},{6,5},{7,4},{8,11},{9,10},{10,... | collective-permute-start | bytes 786440 | tf_op jit(solution)/shard_map/ppermute | solution.py:939
  126.8 22.3 %collective-permute-start.5 = (bf16[3088,128]{1,0:T(8,128)(2,1)S(1)}, bf16[3088,128]{1,0:T(8,128)(2,1)S(1)}, u32[]{:S(2)}, u32[]{:S(2)}) collective-permute-start(bf16[3088,128]{1,0:T(8,128)(2,1)S(1)} %get-tuple-element.141), channel_id=1, source_target_pairs={{0,1},{1,0},{2,3},{3,2},{4,5},{5,4},{6,7},{7,6},{8,9},{9,8},{10,11... | collective-permute-start | bytes 2371592 | tf_op jit(solution)/shard_map/ppermute | solution.py:939
  127.2 19.8 %collective-permute-start.6 = (bf16[3072,128]{1,0:T(8,128)(2,1)S(1)}, bf16[3072,128]{1,0:T(8,128)(2,1)S(1)}, u32[]{:S(2)}, u32[]{:S(2)}) collective-permute-start(bf16[3072,128]{1,0:T(8,128)(2,1)S(1)} %get-tuple-element.142), channel_id=1, source_target_pairs={{0,3},{1,2},{2,1},{3,0},{4,7},{5,6},{6,5},{7,4},{8,11},{9,10},{10,... | collective-permute-start | bytes 2359304 | tf_op jit(solution)/shard_map/ppermute | solution.py:939
  129.2 18.4 %collective-permute-start.7 = (bf16[3072,128]{1,0:T(8,128)(2,1)S(1)}, bf16[3072,128]{1,0:T(8,128)(2,1)S(1)}, u32[]{:S(2)}, u32[]{:S(2)}) collective-permute-start(bf16[3072,128]{1,0:T(8,128)(2,1)S(1)} %get-tuple-element.143), channel_id=1, source_target_pairs={{0,8},{4,12},{8,0},{12,4},{16,24},{20,28},{24,16},{28,20},{32,40},... | collective-permute-start | bytes 2359304 | tf_op jit(solution)/shard_map/ppermute | solution.py:946
  130.9 18.2 %collective-permute-start.8 = (bf16[3072,128]{1,0:T(8,128)(2,1)S(1)}, bf16[3072,128]{1,0:T(8,128)(2,1)S(1)}, u32[]{:S(2)}, u32[]{:S(2)}) collective-permute-start(bf16[3072,128]{1,0:T(8,128)(2,1)S(1)} %get-tuple-element.144), channel_id=1, source_target_pairs={{0,24},{4,28},{8,16},{12,20},{16,8},{20,12},{24,0},{28,4},{32,56},... | collective-permute-start | bytes 2359304 | tf_op jit(solution)/shard_map/ppermute | solution.py:946
  149.6 12.1 %collective-permute-start.9 = (bf16[1552,128]{1,0:T(8,128)(2,1)S(1)}, bf16[1552,128]{1,0:T(8,128)(2,1)S(1)}, u32[]{:S(2)}, u32[]{:S(2)}) collective-permute-start(bf16[1552,128]{1,0:T(8,128)(2,1)S(1)} %get-tuple-element.154), channel_id=1, source_target_pairs={{0,3},{1,2},{2,1},{3,0},{4,7},{5,6},{6,5},{7,4},{8,11},{9,10},{10,... | collective-permute-start | bytes 1191944 | tf_op jit(solution)/shard_map/ppermute | solution.py:939
  150.7 8.7 %collective-permute-start.10 = (bf16[1536,128]{1,0:T(8,128)(2,1)S(1)}, bf16[1536,128]{1,0:T(8,128)(2,1)S(1)}, u32[]{:S(2)}, u32[]{:S(2)}) collective-permute-start(bf16[1536,128]{1,0:T(8,128)(2,1)S(1)} %get-tuple-element.155), channel_id=1, source_target_pairs={{0,1},{1,0},{2,3},{3,2},{4,5},{5,4},{6,7},{7,6},{8,9},{9,8},{10,11... | collective-permute-start | bytes 1179656 | tf_op jit(solution)/shard_map/ppermute | solution.py:939
  151.2 8.7 %collective-permute-start.11 = (bf16[1536,128]{1,0:T(8,128)(2,1)S(1)}, bf16[1536,128]{1,0:T(8,128)(2,1)S(1)}, u32[]{:S(2)}, u32[]{:S(2)}) collective-permute-start(bf16[1536,128]{1,0:T(8,128)(2,1)S(1)} %get-tuple-element.156), channel_id=1, source_target_pairs={{0,24},{4,28},{8,16},{12,20},{16,8},{20,12},{24,0},{28,4},{32,56},... | collective-permute-start | bytes 1179656 | tf_op jit(solution)/shard_map/ppermute | solution.py:946
  152.9 8.9 %collective-permute-start.12 = (bf16[1536,128]{1,0:T(8,128)(2,1)S(1)}, bf16[1536,128]{1,0:T(8,128)(2,1)S(1)}, u32[]{:S(2)}, u32[]{:S(2)}) collective-permute-start(bf16[1536,128]{1,0:T(8,128)(2,1)S(1)} %get-tuple-element.157), channel_id=1, source_target_pairs={{0,8},{4,12},{8,0},{12,4},{16,24},{20,28},{24,16},{28,20},{32,40},... | collective-permute-start | bytes 1179656 | tf_op jit(solution)/shard_map/ppermute | solution.py:946
  162.1 39.0 %copy-start.4 = (f32[2048]{0:T(1024)S(1)}, f32[2048]{0:T(1024)}, u32[]{:S(2)}) copy-start(f32[2048]{0:T(1024)} %param.16) | copy-start | bytes 24580
  162.1 12.2 %collective-permute-start.13 = (bf16[1296,128]{1,0:T(8,128)(2,1)S(1)}, bf16[1296,128]{1,0:T(8,128)(2,1)S(1)}, u32[]{:S(2)}, u32[]{:S(2)}) collective-permute-start(bf16[1296,128]{1,0:T(8,128)(2,1)S(1)} %get-tuple-element.167), channel_id=1, source_target_pairs={{0,8},{4,12},{8,0},{12,4},{16,24},{20,28},{24,16},{28,20},{32,40},... | collective-permute-start | bytes 995336 | tf_op jit(solution)/shard_map/ppermute | solution.py:946
  164.3 7.1 %collective-permute-start.14 = (bf16[1280,128]{1,0:T(8,128)(2,1)S(1)}, bf16[1280,128]{1,0:T(8,128)(2,1)S(1)}, u32[]{:S(2)}, u32[]{:S(2)}) collective-permute-start(bf16[1280,128]{1,0:T(8,128)(2,1)S(1)} %get-tuple-element.168), channel_id=1, source_target_pairs={{0,24},{4,28},{8,16},{12,20},{16,8},{20,12},{24,0},{28,4},{32,56},... | collective-permute-start | bytes 983048 | tf_op jit(solution)/shard_map/ppermute | solution.py:946
  164.5 7.1 %collective-permute-start.15 = (bf16[1280,128]{1,0:T(8,128)(2,1)S(1)}, bf16[1280,128]{1,0:T(8,128)(2,1)S(1)}, u32[]{:S(2)}, u32[]{:S(2)}) collective-permute-start(bf16[1280,128]{1,0:T(8,128)(2,1)S(1)} %get-tuple-element.169), channel_id=1, source_target_pairs={{0,1},{1,0},{2,3},{3,2},{4,5},{5,4},{6,7},{7,6},{8,9},{9,8},{10,11... | collective-permute-start | bytes 983048 | tf_op jit(solution)/shard_map/ppermute | solution.py:939
  166.0 8.3 %collective-permute-start.16 = (bf16[1280,128]{1,0:T(8,128)(2,1)S(1)}, bf16[1280,128]{1,0:T(8,128)(2,1)S(1)}, u32[]{:S(2)}, u32[]{:S(2)}) collective-permute-start(bf16[1280,128]{1,0:T(8,128)(2,1)S(1)} %get-tuple-element.170), channel_id=1, source_target_pairs={{0,3},{1,2},{2,1},{3,0},{4,7},{5,6},{6,5},{7,4},{8,11},{9,10},{10,... | collective-permute-start | bytes 983048 | tf_op jit(solution)/shard_map/ppermute | solution.py:939
  174.3 33.1 %copy-start.3 = (f32[4,1024]{1,0:T(4,128)S(1)}, f32[4,1024]{1,0:T(4,128)}, u32[]{:S(2)}) copy-start(f32[4,1024]{1,0:T(4,128)} %hid_accum_ref.1) | copy-start | bytes 49156
  174.3 33.1 %copy-start.8 = (f32[128]{0:T(128)S(1)}, f32[128]{0:T(128)}, u32[]{:S(2)}) copy-start(f32[128]{0:T(128)} %param.14) | copy-start | bytes 1540
  174.3 33.1 %copy-start.9 = (f32[4]{0:T(128)S(1)}, f32[4]{0:T(128)}, u32[]{:S(2)}) copy-start(f32[4]{0:T(128)} %param.25) | copy-start | bytes 52
  174.6 10.7 %collective-permute-start.17 = (bf16[656,128]{1,0:T(8,128)(2,1)S(1)}, bf16[656,128]{1,0:T(8,128)(2,1)S(1)}, u32[]{:S(2)}, u32[]{:S(2)}) collective-permute-start(bf16[656,128]{1,0:T(8,128)(2,1)S(1)} %get-tuple-element.180), channel_id=1, source_target_pairs={{0,24},{4,28},{8,16},{12,20},{16,8},{20,12},{24,0},{28,4},{32,56},... | collective-permute-start | bytes 503816 | tf_op jit(solution)/shard_map/ppermute | solution.py:946
  176.4 5.3 %collective-permute-start.18 = (bf16[640,128]{1,0:T(8,128)(2,1)S(1)}, bf16[640,128]{1,0:T(8,128)(2,1)S(1)}, u32[]{:S(2)}, u32[]{:S(2)}) collective-permute-start(bf16[640,128]{1,0:T(8,128)(2,1)S(1)} %get-tuple-element.181), channel_id=1, source_target_pairs={{0,8},{4,12},{8,0},{12,4},{16,24},{20,28},{24,16},{28,20},{32,40},... | collective-permute-start | bytes 491528 | tf_op jit(solution)/shard_map/ppermute | solution.py:946
  177.8 6.5 %collective-permute-start.19 = (bf16[640,128]{1,0:T(8,128)(2,1)S(1)}, bf16[640,128]{1,0:T(8,128)(2,1)S(1)}, u32[]{:S(2)}, u32[]{:S(2)}) collective-permute-start(bf16[640,128]{1,0:T(8,128)(2,1)S(1)} %get-tuple-element.182), channel_id=1, source_target_pairs={{0,3},{1,2},{2,1},{3,0},{4,7},{5,6},{6,5},{7,4},{8,11},{9,10},{10,... | collective-permute-start | bytes 491528 | tf_op jit(solution)/shard_map/ppermute | solution.py:939
  180.0 5.3 %collective-permute-start.20 = (bf16[640,128]{1,0:T(8,128)(2,1)S(1)}, bf16[640,128]{1,0:T(8,128)(2,1)S(1)}, u32[]{:S(2)}, u32[]{:S(2)}) collective-permute-start(bf16[640,128]{1,0:T(8,128)(2,1)S(1)} %get-tuple-element.183), channel_id=1, source_target_pairs={{0,1},{1,0},{2,3},{3,2},{4,5},{5,4},{6,7},{7,6},{8,9},{9,8},{10,11... | collective-permute-start | bytes 491528 | tf_op jit(solution)/shard_map/ppermute | solution.py:939
  186.3 21.0 %all-to-all-start.3 = ((bf16[8,336,128]{2,1,0:T(8,128)(2,1)}), bf16[8,336,128]{2,1,0:T(8,128)(2,1)S(1)}, u32[]{:S(2)}, u32[]{:S(2)}) async-start(bf16[8,336,128]{2,1,0:T(8,128)(2,1)} %step_5.1), calls=%async_computation.3 | async-start | bytes 1376256 | tf_op jit(solution)/shard_map/all_to_all | solution.py:953
  193.2 7.6 %collective-permute-start.21 = (bf16[1024,128]{1,0:T(8,128)(2,1)S(1)}, bf16[1024,128]{1,0:T(8,128)(2,1)S(1)}, u32[]{:S(2)}, u32[]{:S(2)}) collective-permute-start(bf16[1024,128]{1,0:T(8,128)(2,1)S(1)} %get-tuple-element.200.a), channel_id=1, source_target_pairs={{0,3},{1,2},{2,1},{3,0},{4,7},{5,6},{6,5},{7,4},{8,11},{9,10},{10,... | collective-permute-start | bytes 786440 | tf_op jit(solution)/shard_map/ppermute | solution.py:939
  194.8 6.4 %collective-permute-start.22 = (bf16[1024,128]{1,0:T(8,128)(2,1)S(1)}, bf16[1024,128]{1,0:T(8,128)(2,1)S(1)}, u32[]{:S(2)}, u32[]{:S(2)}) collective-permute-start(bf16[1024,128]{1,0:T(8,128)(2,1)S(1)} %get-tuple-element.201.c), channel_id=1, source_target_pairs={{0,1},{1,0},{2,3},{3,2},{4,5},{5,4},{6,7},{7,6},{8,9},{9,8},{10,11... | collective-permute-start | bytes 786440 | tf_op jit(solution)/shard_map/ppermute | solution.py:939
  (15 other events, 97.8 us)
